TPU v7x, 128 devices: a whole 4x4x4 slice. The times are simulated.
128 devices in a mesh: expert: 32 (over x, z, core), shard: 4 (over y).
Axes of the slice: x: 4, y: 4, z: 4, core: 2. Of those that a mesh axis runs over, the one named last changes fastest.
Arguments:
- tokens: bfloat16 [16384, 768], P('expert'), may hold values from -6 to 6
- qkv_weight: bfloat16 [3, 768, 768], P(None, None, 'shard'), may hold values from -0.21875 to 0.21875
- out_proj: bfloat16 [768, 768], P('shard'), may hold values from -0.875 to 0.875
- rel_bias: float32 [12, 32], P('shard'), may hold values from -6 to 6
- gains: float32 [2, 768], replicated, may hold values from 0.5 to 1.5
- router: bfloat16 [768, 32], replicated, may hold values from -0.109375 to 0.109375
- w_in: bfloat16 [32, 768, 3072], P('expert', None, 'shard'), may hold values from -0.21875 to 0.21875
- w_out: bfloat16 [32, 3072, 768], P('expert', 'shard'), may hold values from -7 to 7
- route: int32 [16384], P('expert'), may hold values from 0 to 31, as said below
- slot: int32 [16384], P('expert'), may hold values from 0 to 23, as said below
- buckets: int32 [1023], replicated, may hold values from 0 to 31, as said below
- cotangent: bfloat16 [16384, 768], P('expert'), may hold values from -6 to 6
Outputs:
- result: bfloat16 [16384, 768], P('expert')
- grad_tokens: bfloat16 [16384, 768], P('expert')
- grad_qkv: float32 [3, 768, 768], P(None, None, 'shard')
- grad_out_proj: float32 [768, 768], P('shard')
- grad_bias: float32 [12, 32], P('shard')
- grad_gains: float32 [2, 768], replicated
- grad_router: float32 [768, 32], replicated
- grad_w_in: float32 [32, 768, 3072], P('expert', None, 'shard')
- grad_w_out: float32 [32, 3072, 768], P('expert', 'shard')
Inputs may be any that keep to these rules, and one draw needn't show every extreme that they name: Within each aligned block of 512 rows (one sequence) no two rows share both route and slot, and in every block some expert has all 24 slots taken. `slot`: paired with route as stated there. Entry j - i + 511 is the bucket of offset j - i: 0 for offset 0, buckets 0 to 15 for offsets of at most 0 and the rest for positive ones, never falling with the size of the offset within one sign.
All inputs are finite; a program needn't handle non-finite values.
Results may differ from a plain program's by a relative error of at most 0.03.
Values may be sent and summed in bfloat16 or wider, within the bound.
No kernel may reach another device: no remote copies, remote signals or barrier semaphores. Data moves between devices by JAX's collectives and lax.ppermute only.
A program may use at most 128 MiB of HBM per device.

v0:
```python
import jax
import jax.numpy as jnp
from jax import lax
from jax.experimental import pallas as pl
from jax.experimental.pallas import tpu as pltpu
from jax.sharding import PartitionSpec as P

EPS = 1e-06
T = 512
D = 768
NH = 3
HD = 64
W = NH * HD
NE = 32
CAP = 24
SLOTS = NE * CAP
NS = 4
SCALE = HD ** (-0.5)
f32 = jnp.float32
b16 = jnp.bfloat16

NN = (((1,), (0,)), ((), ()))
NT = (((1,), (1,)), ((), ()))
TN = (((0,), (0,)), ((), ()))


def dot(a, b, dims=NN):
    return lax.dot_general(a, b, dims, preferred_element_type=f32)


class Place:
    def __init__(self, axis):
        self.axis = axis


class Parts:
    def __init__(self, array):
        self.array = array


class Quarter:
    def __init__(self, array):
        self.array = array


class Pieces:
    def __init__(self, arrays, first=0, rows=None):
        self.arrays = arrays
        self.first, self.rows = first, arrays[0].shape[0] if rows is None else rows


class Hold:
    def __init__(self, array):
        self.array = array


class Load:
    def __init__(self, held, copies):
        self.held, self.copies = held, copies

    def start(self):
        for c in self.copies:
            c.start()

    def ready(self, at=None):
        for k, c in enumerate(self.copies):
            if c is not None and (at is None or at == k):
                c.wait()
                self.copies[k] = None

    def __getitem__(self, at):
        self.ready()
        return self.held[at]


class LoadParts(Load):
    def __getitem__(self, at):
        self.ready(at if isinstance(at, int) else at[0])
        return self.held[at]


class Store:
    def __init__(self, out, held, sems):
        self.out, self.held, self.sems, self.copies = out, held, sems, []

    def __setitem__(self, at, value):
        self.held[at] = value

    def flush(self, at=None, src=None):
        sem = self.sems.at[len(self.copies)]
        src = self.held if src is None else src
        if at is None:
            copy = pltpu.make_async_copy(src, self.out, sem)
        else:
            copy = pltpu.make_async_copy(src.at[at], self.out.at[at], sem)
        copy.start()
        self.copies.append(copy)

    def send(self, src, at):
        copy = pltpu.make_async_copy(src, self.out.at[at], self.sems.at[len(self.copies)])
        copy.start()
        self.copies.append(copy)

    def finish(self):
        for c in self.copies:
            c.wait()


def call(body, outs, *args, name, scratch=(), unheld=(), room=0):
    outs = [jax.ShapeDtypeStruct(s, t) for s, t in outs]
    hbm = pl.BlockSpec(memory_space=pltpu.HBM)
    flat, in_specs, buffers = [], [], []
    for a in args:
        if isinstance(a, Place):
            continue
        if isinstance(a, Pieces):
            flat += a.arrays
            in_specs += [hbm] * NS
            shape = (NS, a.rows) + a.arrays[0].shape[1:]
            buffers += [pltpu.VMEM(shape, a.arrays[0].dtype), pltpu.SemaphoreType.DMA((NS,))]
        elif isinstance(a, Parts):
            flat.append(a.array)
            in_specs.append(hbm)
            buffers += [pltpu.VMEM(a.array.shape, a.array.dtype), pltpu.SemaphoreType.DMA((a.array.shape[0],))]
        elif isinstance(a, Quarter):
            flat.append(a.array)
            in_specs.append(hbm)
            shape = (a.array.shape[0] // NS,) + a.array.shape[1:]
            buffers += [pltpu.VMEM(shape, a.array.dtype), pltpu.SemaphoreType.DMA((1,))]
        else:
            held = isinstance(a, Hold)
            flat.append(a.array if held else a)
            in_specs.append(hbm)
            buffers += [] if held else [pltpu.VMEM(a.shape, a.dtype), pltpu.SemaphoreType.DMA((1,))]
    for k, o in enumerate(outs):
        if k not in unheld:
            buffers.append(pltpu.VMEM(o.shape, o.dtype))
        buffers.append(pltpu.SemaphoreType.DMA((4,)))

    def kernel(*refs):
        ins = iter(refs[: len(flat)])
        results = refs[len(flat) : len(flat) + len(outs)]
        rest = refs[len(flat) + len(outs) :]
        bufs, user = iter(rest[: len(buffers)]), rest[len(buffers) :]
        given, me = [], None
        for a in args:
            if isinstance(a, Place):
                me = [lax.axis_index(a.axis)]
                given.append(me)
                continue
            if isinstance(a, Hold):
                given.append(next(ins))
                continue
            if isinstance(a, Pieces):
                held, sems = next(bufs), next(bufs)
                cut = pl.ds(a.first, a.rows)
                item = Load(held, [
                    pltpu.make_async_copy(next(ins).at[cut], held.at[lax.rem(me[0] + (NS - d), NS)], sems.at[d])
                    for d in range(NS)
                ])
            elif isinstance(a, Parts):
                ref, held, sems = next(ins), next(bufs), next(bufs)
                item = LoadParts(held, [
                    pltpu.make_async_copy(ref.at[k], held.at[k], sems.at[k]) for k in range(a.array.shape[0])
                ])
            elif isinstance(a, Quarter):
                ref, held, sems = next(ins), next(bufs), next(bufs)
                n = held.shape[0]
                at = pl.ds(pl.multiple_of(me[0] * n, n), n)
                item = Load(held, [pltpu.make_async_copy(ref.at[at], held, sems.at[0])])
            else:
                ref, held, sems = next(ins), next(bufs), next(bufs)
                item = Load(held, [pltpu.make_async_copy(ref, held, sems.at[0])])
            item.start()
            given.append(item)
        stores = []
        for k, out in enumerate(results):
            held = None if k in unheld else next(bufs)
            stores.append(Store(out, held, next(bufs)))
        body(*given, *stores, *user)
        for item in given:
            if isinstance(item, Load):
                item.ready()
        for item in stores:
            if not item.copies:
                item.flush()
        for item in stores:
            item.finish()

    return pl.pallas_call(
        kernel,
        out_shape=outs,
        in_specs=in_specs,
        out_specs=[hbm] * len(outs),
        scratch_shapes=buffers + list(scratch),
        compiler_params=pltpu.CompilerParams(vmem_limit_bytes=(60 - room) * 1024 * 1024),
        cost_estimate=pl.CostEstimate(flops=0, bytes_accessed=300000, transcendentals=0),
        name=name,
    )(*flat)


def lanes(shape):
    return lax.broadcasted_iota(jnp.int32, shape, len(shape) - 1)


def rows_of(shape):
    return lax.broadcasted_iota(jnp.int32, shape, len(shape) - 2)


def roll_half(v):
    return pltpu.roll(v, 64, v.ndim - 1)


def inv_rms(v):
    return lax.rsqrt(jnp.mean(v * v, axis=-1, keepdims=True) + EPS)


def toeplitz_rows(offsets_row, rows, shift):
    wide = jnp.broadcast_to(offsets_row, (rows, offsets_row.shape[1]))
    return pltpu.roll(wide, shift, 1, stride=1, stride_axis=0)


def bucket_hot(bk):
    return (bk == rows_of((NE, 1024))).astype(f32)


def pack_rows(block, half):
    low = lanes((T // 2, 128)) < 64
    tail = jnp.where(low, half[: T // 2], roll_half(half[T // 2 :]))
    return jnp.concatenate([block, tail], axis=0).astype(b16)


def unpack_rows(pieces):
    low = lanes((T // 2, 128)) < 64
    blocks = [p[:T] for p in pieces]
    for left, right in ((0, 1), (2, 3)):
        l_half = pieces[left][T:].astype(f32)
        r_half = pieces[right][T:].astype(f32)
        top = jnp.where(low, l_half, roll_half(r_half))
        bottom = jnp.where(low, roll_half(l_half), r_half)
        blocks.append(jnp.concatenate([top, bottom], axis=0).astype(b16))
    return jnp.concatenate(blocks, axis=1)


def dispatch_body(route, slot, val, out):
    hot = (route[...] * CAP + slot[...] == rows_of((SLOTS, T))).astype(b16)
    out[...] = dot(hot, val[...]).reshape(NE, CAP, D).astype(b16)


def attend_body(tok, gains, w, rb, bk, heads, heads_t, a_out, qk_t, v_out, p_out):
    x = tok[...].astype(f32)
    a = (x * inv_rms(x) * gains[0:1, :]).astype(b16)
    a_out[...] = a
    a_out.flush()
    q_t = dot(w[0], a, NT).astype(b16)
    v_t = dot(w[2], a, NT).astype(b16)
    k = dot(a, w[1], NT).astype(b16)
    qk_t[0] = q_t
    qk_t[1] = dot(w[1], a, NT).astype(b16)
    qk_t.flush()
    v_out[...] = dot(a, w[2], NT).astype(b16)
    v_out.flush()
    off = lax.dot_general(rb[...], bucket_hot(bk[...]), NN, precision=lax.Precision.HIGHEST, preferred_element_type=f32)
    outs = []
    for h in range(NH):
        part = slice(HD * h, HD * h + HD)
        s = dot(k[:, part], q_t[part]) * SCALE
        wide = toeplitz_rows(off[h : h + 1], 128, 897)
        bias = jnp.concatenate([wide[:, 384 - 128 * b : 896 - 128 * b] for b in range(4)], axis=0)
        s = s + bias
        e = jnp.exp(s - jnp.max(s, axis=0, keepdims=True))
        p = e / jnp.sum(e, axis=0, keepdims=True)
        p_out[h] = p
        p_out.flush(h)
        outs.append(dot(v_t[part], p.astype(b16)))
    heads_t[...] = jnp.concatenate(outs, axis=0).astype(b16)
    block = jnp.concatenate(outs[:2], axis=0).T
    tail = jnp.concatenate([outs[2][:, : T // 2], outs[2][:, T // 2 :]], axis=0).T
    heads[...] = jnp.concatenate([block, tail], axis=0).astype(b16)


def order_weights_body(me, held, out):
    parts = [held[j, :128] for j in range(NS)] + [held[j, 128:] for j in range(NS)]
    out[...] = jnp.concatenate(parts, axis=0)


def mix_body(me, route, slot, gains, held, w, tok, rows, u_out, hidden_out):
    full = unpack_rows([held[j] for j in range(NS)])
    hidden = tok[...].astype(f32) + dot(full, w[...])
    u = (hidden * inv_rms(hidden) * gains[1:2, :]).astype(b16)
    hidden_out[...] = hidden
    hidden_out.flush()
    u_out[...] = u
    u_out.flush()
    hot = (route[...] * CAP + slot[...] == rows_of((SLOTS, T))).astype(b16)
    rows[...] = dot(hot, u).reshape(NE, CAP, D).astype(b16)


def gate_body(u, router, route, slot, gate_out, coef_out, index_out):
    index_out[...] = route[...] * CAP + slot[...]
    logits = dot(u[...], router[...], NT)
    e = jnp.exp(logits - jnp.max(logits, axis=1, keepdims=True))
    probs = e / jnp.sum(e, axis=1, keepdims=True)
    chosen = (route[...] == lanes((T, NE))).astype(f32)
    gate = jnp.sum(probs * chosen, axis=1, keepdims=True)
    coef = probs * (chosen - gate)
    gate_out[...] = gate
    coef_out[...] = coef


def ungated_body(g, w_out, h):
    h[...] = dot(g[...], w_out[...], NT)


def pack_return(val, extra=None):
    n = val.shape[0] // CAP
    low = lanes((n, 8, 128)) < 64
    if extra is not None:
        ext = extra.reshape(n, CAP, 1)
        hi = ext.astype(b16).astype(f32)
        lo = ext - hi
        lane = lanes((n, 8, 128))
        tail = jnp.zeros((n, 8, 128), f32)
        for t in range(3):
            tail = jnp.where(lane == 64 + t, hi[:, 8 * t : 8 * t + 8], tail)
            tail = jnp.where(lane == 67 + t, lo[:, 8 * t : 8 * t + 8], tail)
    else:
        tail = jnp.zeros((n, 8, 128), f32)
    res = []
    for s in range(NS):
        block = val[:, 128 * s : 128 * s + 128].reshape(n, CAP, 128)
        c = 512 + 128 * (s // 2)
        half = val[:, c : c + 128].reshape(n, CAP, 128)
        moved = roll_half(half)
        x0, x1, x2 = (half[:, 8 * t : 8 * t + 8] for t in range(3))
        r0, r1, r2 = (moved[:, 8 * t : 8 * t + 8] for t in range(3))
        if s % 2 == 0:
            t3, t4 = jnp.where(low, x0, r1), jnp.where(low, x2, tail)
        else:
            t3, t4 = jnp.where(low, r0, x1), jnp.where(low, r2, tail)
        res.append(jnp.concatenate([block, t3, t4], axis=1))
    return [r.astype(b16) for r in res]


MAIN = 144
PAY = 160

GELU_C = 0.7978845608028654


def expert_body(me, router, rows, w_in, h, ret, act_out, dpre_out, gate_out):
    half = SLOTS // 2
    for i in range(2):
        cut = slice(half * i, half * i + half)
        seqs = slice(NE // 2 * i, NE // 2 * (i + 1))
        u = rows[cut, :]
        logits = dot(u, router[...], NT)
        e = jnp.exp(logits - jnp.max(logits, axis=1, keepdims=True))
        mine = (lanes(logits.shape) == me[0]).astype(f32)
        gate = jnp.sum(e * mine, axis=1, keepdims=True) / jnp.sum(e, axis=1, keepdims=True)
        pre = dot(u, w_in[...])
        sq = pre * pre
        th = jnp.tanh(GELU_C * pre * (1.0 + 0.044715 * sq))
        act = (0.5 * pre * (1.0 + th)).astype(b16)
        slope = 0.5 * (1.0 + th) + 0.5 * pre * (1.0 - th * th) * (GELU_C * (1.0 + 3 * 0.044715 * sq))
        hv = h[cut, :]
        d_gate = jnp.sum(act.astype(f32) * hv, axis=1, keepdims=True)
        d_pre = (gate * hv * slope).astype(b16)
        grads = pack_return(dot(d_pre, w_in[...], NT), d_gate)
        for s in range(NS):
            ret[seqs, s] = grads[s]
        ret.flush(seqs)
        act_out[cut, :] = act
        dpre_out[cut, :] = d_pre
        gate_out[cut, :] = gate


def value_body(act, w_out, out):
    out[...] = dot(act[...], w_out[...]).reshape(NE, CAP, D).astype(b16)


def unpack_return(total):
    block = total[:, :CAP].reshape(SLOTS, 128).astype(b16)
    t3 = total[:, 24:32]
    t4 = total[:, 32:40]
    return block, jnp.concatenate([t3, roll_half(t3), t4], axis=1).reshape(SLOTS, 128), t4


def collect_body(index, got, piece, d_gate):
    block, half, t4 = unpack_return(jnp.sum(got[...].astype(f32), axis=1))
    lane = lanes((SLOTS, 128))
    tl = lanes(t4.shape)
    cols = []
    for t in range(3):
        cols.append(jnp.sum(jnp.where((tl == 64 + t) | (tl == 67 + t), t4, 0.0), axis=2, keepdims=True))
    col = jnp.concatenate(cols, axis=1).reshape(SLOTS, 1)
    hi = col.astype(b16).astype(f32)
    half = jnp.where(lane < 64, half, jnp.where(lane == 64, hi, jnp.where(lane == 65, col - hi, 0.0)))
    hot = (index[...] == lanes((T, SLOTS))).astype(b16)
    mine = dot(hot, jnp.concatenate([block, half.astype(b16)], axis=1))
    piece[...] = pack_rows(mine[:, :128], mine[:, 128:])
    piece.flush()
    lt = lanes((T, 128))
    d_gate[...] = jnp.sum(jnp.where((lt == 64) | (lt == 65), mine[:, 128:], 0.0), axis=1, keepdims=True)


def backward_body(
    me, gains, d_gate, coef, router, held, hidden_in, cot, out_proj, v, p, qk_t, heads_t, u, a, bk, w,
    pay, d_proj, gain_out, dhid_out, scr, dhid,
):
    d_expert = unpack_rows([held[j] for j in range(NS)]).astype(f32)
    dg = d_gate[...]
    d_logits = coef[...] * dg
    high = d_logits.astype(b16)
    low = (d_logits - high.astype(f32)).astype(b16)
    d_u = dot(high, router[...]) + dot(low, router[...]) + d_expert
    hidden = hidden_in[...]
    r2 = inv_rms(hidden)
    n2 = hidden * r2
    gain_two = jnp.sum(d_u * n2, axis=0, keepdims=True)
    v2 = d_u * gains[1:2, :]
    d_hidden = cot[...].astype(f32) + r2 * (v2 - n2 * jnp.mean(v2 * n2, axis=-1, keepdims=True))
    dhid[...] = d_hidden
    dhid_out.flush(src=dhid.at[pl.ds(pl.multiple_of(me[0] * 128, 128), 128)])
    d_att = d_hidden.astype(b16)
    router_t = dot(high, u[...], TN) + dot(low, u[...], TN)
    g_out = dot(heads_t[...], d_att)
    do_t = dot(out_proj[...], d_att, NT).astype(b16)
    hot = bucket_hot(bk[...])
    dqs, dks, dvs, bias = [], [], [], []
    for h in range(NH):
        part = slice(HD * h, HD * h + HD)
        prob = p[h]
        dp = dot(v[:, part], do_t[part])
        delta = jnp.sum(prob * dp, axis=0, keepdims=True)
        ds = (prob * (dp - delta)).astype(b16)
        dvs.append(dot(do_t[part], prob.astype(b16), NT))
        dks.append(dot(qk_t[0, part], ds, NT) * SCALE)
        dqs.append(dot(qk_t[1, part], ds) * SCALE)
        ds_f = ds.astype(f32)
        acc = jnp.zeros((128, 1024), f32)
        for b in range(4):
            left, right = 384 - 128 * b, 128 + 128 * b
            blk = ds_f[128 * b : 128 * b + 128]
            parts = ([jnp.zeros((128, left), f32)] if left else []) + [blk, jnp.zeros((128, right), f32)]
            acc = acc + jnp.concatenate(parts, axis=1)
        for step in (64, 32, 16, 8):
            acc = acc[:step] + pltpu.roll(acc[step:], 1024 - step, 1)
        row = rows_of((8, 1024))
        for step in (4, 2, 1):
            acc = jnp.where((row & step) != 0, pltpu.roll(acc, 1024 - step, 1), acc)
        bias.append(pltpu.roll(jnp.sum(acc, axis=0, keepdims=True), 127, 1))
    bias = lax.dot_general(
        jnp.concatenate(bias + [jnp.zeros((5, 1024), f32)], axis=0), hot, NT,
        precision=lax.Precision.HIGHEST, preferred_element_type=f32,
    )
    dq = jnp.concatenate(dqs, axis=0).astype(b16)
    dk = jnp.concatenate(dks, axis=0).astype(b16)
    dv = jnp.concatenate(dvs, axis=0).astype(b16)
    for c, m in enumerate((dq, dk, dv)):
        d_proj[c] = m
    d_proj.flush()
    a_v = a[...]
    grads = [dot(m, a_v) for m in (dq, dk, dv)]
    gain_rows = [
        jnp.sum(w[c].astype(f32) * grads[c], axis=0, keepdims=True) for c in range(3)
    ]
    gain_one = gain_rows[0] + gain_rows[1] + gain_rows[2]
    full = jnp.concatenate([g.astype(b16) for g in grads + [g_out]], axis=0)
    big = jnp.concatenate([full[:, 128 * l : 128 * l + 128] for l in range(6)], axis=0)
    for c in range(NE):
        pay[c, :MAIN] = big[MAIN * c : MAIN * c + MAIN]
    scr[:, 6:, :] = jnp.zeros((NE, 10, 128), f32)
    wide = jnp.concatenate([bias, jnp.zeros((8, 96), f32)], axis=1)
    for l in range(6):
        scr[:, l, :] = router_t[:, 128 * l : 128 * l + 128]
        scr[l, 6:7, :] = gain_two[:, 128 * l : 128 * l + 128]
    for h in range(NH):
        scr[6 + h, 6:7, :] = wide[h : h + 1]
    pay[:, MAIN:, :] = scr[...].astype(b16)
    gain_out[...] = gain_one


def input_grad_body(me, gain, index, got, d_proj, w, da0, da1, da2, da3, grads, values):
    hot = (index[...] == lanes((T, SLOTS))).astype(b16)
    values[...] = dot(hot, got[...])
    grads[...] = dot(d_proj[0], w[0], TN) + dot(d_proj[1], w[1], TN) + dot(d_proj[2], w[2], TN)
    one = gain[...]
    hi = one.astype(b16).astype(f32)
    gl = jnp.concatenate([hi, one - hi, jnp.zeros((14, D), f32)], axis=0).astype(b16)
    for d, out in enumerate((da0, da1, da2, da3)):
        to = pl.ds(pl.multiple_of(lax.rem(me[0] + d, NS) * 128, 128), 128)
        out[:128] = grads[to, :].astype(b16)
        out[128:144] = gl
        out[144:] = values[to, :].astype(b16)
        out.flush()


def sum_body(me, held, pay, out):
    total = jnp.sum(pay[...].astype(f32), axis=0)
    gl = jnp.sum(jnp.sum(held[...].astype(f32), axis=0), axis=0, keepdims=True)
    gl = [gl[:, 128 * l : 128 * l + 128] for l in range(6)] + [jnp.zeros((2, 128), f32)]
    chunk = jnp.concatenate([total[: MAIN + 8]] + gl, axis=0).astype(b16)
    out[...] = jnp.broadcast_to(chunk[None], (NE, PAY, 128))


def token_grad_body(me, gains, held, tok, dhid, gate, hidden, out):
    d_a = jnp.sum(held[:, :128, :].astype(f32), axis=0)
    x = tok[...].astype(f32)
    r1 = inv_rms(x)
    n1 = x * r1
    v1 = d_a * gains[0:1, :]
    grad = dhid[...] + r1 * (v1 - n1 * jnp.mean(v1 * n1, axis=-1, keepdims=True))
    value = jnp.sum(held[:, 144:, :].astype(f32), axis=0).astype(b16).astype(f32)
    out[:128] = (hidden[...] + gate[...] * value).astype(b16)
    out[128:] = grad.astype(b16)


def tokens_body(me, held, result, grad):
    held.ready()
    for j in range(NS):
        rows = pl.ds(128 * j, 128)
        result.send(held.held.at[j, pl.ds(0, 128)], rows)
        grad.send(held.held.at[j, pl.ds(128, 128)], rows)


def finish_body(got, gains, qkv, proj, bias, gains_out, router, scr):
    big = jnp.concatenate([got[c, :MAIN] for c in range(NE)], axis=0)
    full = jnp.concatenate([big[D * l : D * l + D] for l in range(6)], axis=1)
    for c in range(3):
        qkv[c] = full[W * c : W * c + W].astype(f32)
        qkv.flush(c)
    proj[...] = full[3 * W :].astype(f32)
    proj.flush()
    scr[...] = got[:, MAIN:, :].astype(f32)
    router[...] = jnp.concatenate([scr[:, l, :] for l in range(6)], axis=1)
    gl = jnp.sum(scr[:, 8:, :], axis=0)
    one = jnp.concatenate([gl[l : l + 1] for l in range(6)], axis=1) / gains[0:1, :]
    two = jnp.concatenate([scr[l, 6:7, :] for l in range(6)], axis=1)
    gains_out[...] = jnp.concatenate([one, two], axis=0)
    bias[...] = jnp.concatenate([scr[6 + h, 6:7, :NE] for h in range(NH)], axis=0)


def over_experts(v):
    return lax.all_to_all(v, "expert", split_axis=0, concat_axis=0, tiled=True)


def over_all(v):
    return lax.all_to_all(v, ("expert", "shard"), split_axis=0, concat_axis=0, tiled=True)


def rotate(v, d):
    return lax.ppermute(v, "shard", [(i, (i + d) % NS) for i in range(NS)])


def round_shard(v):
    return [v] + [rotate(v, d) for d in (1, 2, 3)]


def local(tokens, qkv_weight, out_proj, rel_bias, gains, router, w_in, w_out, route, slot, buckets, cotangent):
    w_in = w_in.reshape(D, -1)
    w_out = w_out.reshape(-1, D)
    ff = w_in.shape[1]
    me, expert = Place("shard"), Place("expert")
    route_row, slot_row = route[None, :], slot[None, :]
    bk = jnp.concatenate([jnp.flip(buckets), jnp.full((1,), -1, jnp.int32)])[None, :]
    w_t = jnp.transpose(qkv_weight, (0, 2, 1))
    router_t = router.T
    together = lax.optimization_barrier

    (g_rows,) = call(dispatch_body, [((NE, CAP, D), b16)], route_row, slot_row, cotangent, name="dispatch_cotangent")
    g_rows = over_experts(g_rows).reshape(SLOTS, D)
    w_pieces = round_shard(out_proj)
    heads, heads_t, a, qk_t, v, p = call(
        attend_body,
        [((D, 128), b16), ((W, T), b16), ((T, D), b16), ((2, W, T), b16), ((T, W), b16), ((NH, T, T), f32)],
        tokens, gains, Parts(w_t), rel_bias, bk, name="attend",
    )
    h_pieces = round_shard(heads)
    (w_full,) = call(order_weights_body, [((D, D), b16)], me, Pieces(w_pieces), name="order_weights", room=25)
    rows, u, hidden = call(
        mix_body,
        [((NE, CAP, D), b16), ((T, D), b16), ((T, D), f32)],
        me, route_row, slot_row, gains, Pieces(h_pieces), w_full, tokens, name="mix",
    )
    u_rows = over_experts(rows).reshape(SLOTS, D)
    (h,) = call(ungated_body, [((SLOTS, ff), f32)], g_rows, w_out, name="ungated")
    gate, coef, index = call(
        gate_body, [((T, 1), f32), ((T, NE), f32), ((T, 1), jnp.int32)], u, router_t, route[:, None], slot[:, None],
        name="gate",
    )
    u_rows, h, gate, coef, index = together((u_rows, h, gate, coef, index))
    ret, act, d_pre, row_gate = call(
        expert_body,
        [((NE, NS, 40, 128), b16), ((SLOTS, ff), b16), ((SLOTS, ff), b16), ((SLOTS, 1), f32)],
        expert, router_t, u_rows, w_in, h, name="expert",
    )
    back = over_all(ret.reshape(NE * NS, 40, 128)).reshape(NE, NS, 40, 128)
    (val,) = call(value_body, [((NE, CAP, D), b16)], act, w_out, name="value")
    d_rows = (row_gate * g_rows.astype(f32)).astype(b16)
    grad_w_out = dot(act, d_rows, TN)
    grad_w_in = dot(u_rows, d_pre, TN)
    back, val, grad_w_out, grad_w_in = together((back, val, grad_w_out, grad_w_in))
    piece, d_gate = call(
        collect_body, [((D, 128), b16), ((T, 1), f32)], index, back, name="collect_back", room=25
    )
    b_pieces = round_shard(piece)
    value = over_experts(val).reshape(SLOTS, D)
    pay, d_proj, gain_one, d_hidden = call(
        backward_body,
        [((NE, PAY, 128), b16), ((3, W, T), b16), ((1, D), f32), ((T // NS, D), f32)],
        me, gains, d_gate, coef, router_t, Pieces(b_pieces), hidden, cotangent, out_proj, v, Parts(p), qk_t, heads_t, u,
        a, bk, w_t, name="backward", unheld=(3,),
        scratch=[pltpu.VMEM((NE, 16, 128), f32), pltpu.VMEM((T, D), f32)],
    )
    pay, value, d_proj, gain_one = together((pay, value, d_proj, gain_one))
    pay = over_experts(pay)
    da = call(
        input_grad_body, [((272, D), b16)] * NS, me, gain_one, index, value, d_proj, w_t, name="input_grad",
        scratch=[pltpu.VMEM((T, D), f32), pltpu.VMEM((T, D), f32)],
    )
    da = [da[0]] + [rotate(x, d) for d, x in enumerate(da) if d]
    (t_piece,) = call(
        token_grad_body, [((256, D), b16)], me, gains, Pieces(da), Quarter(tokens), d_hidden,
        Quarter(gate), Quarter(hidden), name="token_grad",
    )
    (chunk,) = call(sum_body, [((NE, PAY, 128), b16)], me, Pieces(da, 128, 16), pay, name="sum_gradients", room=25)
    chunk = over_experts(chunk)
    result, grad_tokens = call(
        tokens_body, [((T, D), b16), ((T, D), b16)], me, Pieces(round_shard(t_piece)), name="tokens", room=25,
        unheld=(0, 1),
    )
    chunk, grad_tokens, result = together((chunk, grad_tokens, result))
    grad_qkv, grad_proj, grad_bias, grad_gains, grad_router = call(
        finish_body,
        [((3, W, D), f32), ((W, D), f32), ((NH, NE), f32), ((2, D), f32), ((NE, D), f32)],
        chunk, gains, name="finish", room=25, scratch=[pltpu.VMEM((NE, 16, 128), f32)],
    )
    grad_qkv = jnp.transpose(grad_qkv, (0, 2, 1))
    return (
        result, grad_tokens, grad_qkv, grad_proj, grad_bias, grad_gains, grad_router.T, grad_w_in[None],
        grad_w_out[None],
    )


def solution(mesh):
    in_specs = (
        P("expert", None),
        P(None, None, "shard"),
        P("shard", None),
        P("shard", None),
        P(),
        P(),
        P("expert", None, "shard"),
        P("expert", "shard", None),
        P("expert"),
        P("expert"),
        P(),
        P("expert", None),
    )
    out_specs = (
        P("expert", None),
        P("expert", None),
        P(None, None, "shard"),
        P("shard", None),
        P("shard", None),
        P(),
        P(),
        P("expert", None, "shard"),
        P("expert", "shard", None),
    )
    return jax.shard_map(local, mesh=mesh, in_specs=in_specs, out_specs=out_specs, check_vma=False)
```

profile of v0, /device:TPU:0, one launch (start us, length us, event | category | flops | bytes accessed | tf_op | source)
XLA Modules:
  0.0 217.0 jit_solution(7033042375960368257)
XLA Ops:
  0.6 3.0 %dispatch_cotangent.1 = bf16[32,24,768]{2,1,0:T(8,128)(2,1)} custom-call(s32[1,512]{1,0:T(1,128)} %bitcast.40, s32[1,512]{1,0:T(1,128)} %bitcast.43, bf16[512,768]{1,0:T(8,128)(2,1)} %refs_9_.1), custom_call_target="tpu_custom_call" | custom-call | bytes 300000 | tf_op jit(solution)/shard_map/dispatch_cotangent/pallas_call | solution.py:190
  3.7 8.4 %all-to-all-start.1 = ((bf16[32,24,768]{2,1,0:T(8,128)(2,1)}), bf16[32,24,768]{2,1,0:T(8,128)(2,1)S(1)}, u32[]{:S(2)}, u32[]{:S(2)}) async-start(bf16[32,24,768]{2,1,0:T(8,128)(2,1)} %dispatch_cotangent.1), calls=%async_computation.1 | async-start | bytes 2359296 | tf_op jit(solution)/shard_map/all_to_all | solution.py:545
  12.1 1.6 collective-permute-start.3
  13.8 2.9 %collective-permute-start.4 = (bf16[192,768]{1,0:T(8,128)(2,1)S(1)}, bf16[192,768]{1,0:T(8,128)(2,1)S(1)}, u32[]{:S(2)}, u32[]{:S(2)}) collective-permute-start(bf16[192,768]{1,0:T(8,128)(2,1)S(1)} %copy-done.6), channel_id=1, source_target_pairs={{0,2},{1,3},{2,0},{3,1},{4,6},{5,7},{6,4},{7,5},{8,10},{9,11},{10,... | collective-permute-start | bytes 884744 | tf_op jit(solution)/shard_map/ppermute | solution.py:553
  16.7 1.3 collective-permute-start.5
  18.8 6.9 %attend.1 = (bf16[768,128]{1,0:T(8,128)(2,1)}, bf16[192,512]{1,0:T(8,128)(2,1)}, bf16[512,768]{1,0:T(8,128)(2,1)}, bf16[2,192,512]{2,1,0:T(8,128)(2,1)}, bf16[51...) custom-call(bf16[512,768]{1,0:T(8,128)(2,1)} %refs_5_.1, f32[2,768]{1,0:T(2,128)} %refs_1_.3, bf16[3,192,768]{2,1,0:T(8,128)(2,1)} %bitcast.23, ...), custom_call_target="tpu_custom_call" | custom-call | bytes 300000 | tf_op jit(solution)/shard_map/attend/pallas_call | solution.py:190
  27.3 2.0 collective-permute-start.2
  29.3 1.5 collective-permute-done.4.refs_2_
  31.5 1.0 copy-done
  32.5 2.5 %collective-permute-done.refs_4_ = bf16[768,128]{1,0:T(8,128)(2,1)S(1)} collective-permute-done((bf16[768,128]{1,0:T(8,128)(2,1)}, bf16[768,128]{1,0:T(8,128)(2,1)S(1)}, u32[]{:S(2)}, u32[]{:S(2)}) %collective-permute-start) | collective-permute-done | bytes 196640 | tf_op jit(solution)/shard_map/ppermute | solution.py:553
  35.0 3.6 %collective-permute-done.1.refs_5_ = bf16[768,128]{1,0:T(8,128)(2,1)S(1)} collective-permute-done((bf16[768,128]{1,0:T(8,128)(2,1)}, bf16[768,128]{1,0:T(8,128)(2,1)S(1)}, u32[]{:S(2)}, u32[]{:S(2)}) %collective-permute-start.1) | collective-permute-done | bytes 196640 | tf_op jit(solution)/shard_map/ppermute | solution.py:553
  39.9 5.7 %mix.1 = (bf16[32,24,768]{2,1,0:T(8,128)(2,1)}, bf16[512,768]{1,0:T(8,128)(2,1)}, f32[512,768]{1,0:T(8,128)}) custom-call(s32[1,512]{1,0:T(1,128)} %bitcast.41, s32[1,512]{1,0:T(1,128)} %bitcast.44, f32[2,768]{1,0:T(2,128)} %refs_1_.3, bf16[768,128]{1,0:T(8,128)(2,1)} %get-tuple-element.58.refs_3_, bf16[768,128]{1,0:T(8,128)(2,1)} %copy-done.18, ...), custom_call_target="tpu_custom_call" | custom-call | bytes 300000 | tf_op jit(solution)/shard_map/mix/pallas_call | solution.py:190
  45.6 1.0 copy-done.12
  46.6 7.4 %all-to-all-start = ((bf16[32,24,768]{2,1,0:T(8,128)(2,1)}), bf16[32,24,768]{2,1,0:T(8,128)(2,1)S(1)}, u32[]{:S(2)}, u32[]{:S(2)}) async-start(bf16[32,24,768]{2,1,0:T(8,128)(2,1)} %get-tuple-element.59), calls=%async_computation | async-start | bytes 2359296 | tf_op jit(solution)/shard_map/all_to_all | solution.py:545
  54.1 0.9 copy.21.refs_2_
  54.9 0.9 copy.22.refs_3_
  55.8 2.9 %gate.1 = (f32[512,1]{1,0:T(8,128)}, f32[512,32]{1,0:T(8,128)}, s32[512,1]{1,0:T(8,128)}) custom-call(bf16[512,768]{1,0:T(8,128)(2,1)} %get-tuple-element.60.refs_0_.refs_15_, bf16[32,768]{1,0:T(8,128)(2,1)} %bitcast.35, s32[512,1]{1,0:T(8,128)} %copy.21.refs_2_, s32[512,1]{1,0:T(8,128)} %copy.22.refs_3_), custom_call_target="tpu_custom_call" | custom-call | bytes 300000 | tf_op jit(solution)/shard_map/gate/pallas_call | solution.py:190
  58.7 4.2 %ungated.1.refs_3_ = f32[768,768]{1,0:T(8,128)} custom-call(bf16[768,768]{1,0:T(8,128)(2,1)} %bitcast.29, bf16[768,768]{1,0:T(8,128)(2,1)} %bitcast.26), custom_call_target="tpu_custom_call" | custom-call | bytes 300000 | tf_op jit(solution)/shard_map/ungated/pallas_call | solution.py:190
  62.9 9.3 %all-to-all-done = bf16[32,24,768]{2,1,0:T(8,128)(2,1)S(1)} async-done(((bf16[32,24,768]{2,1,0:T(8,128)(2,1)}), bf16[32,24,768]{2,1,0:T(8,128)(2,1)S(1)}, u32[]{:S(2)}, u32[]{:S(2)}) %all-to-all-start) | async-done | bytes 1179680 | tf_op jit(solution)/shard_map/all_to_all | solution.py:545
  72.3 1.0 copy-done.14
  73.3 7.2 %expert.1 = (bf16[32,4,40,128]{3,2,1,0:T(8,128)(2,1)}, bf16[768,768]{1,0:T(8,128)(2,1)}, bf16[768,768]{1,0:T(8,128)(2,1)}, f32[768,1]{1,0:T(8,128)}) custom-call(bf16[32,768]{1,0:T(8,128)(2,1)} %bitcast.36, bf16[768,768]{1,0:T(8,128)(2,1)} %bitcast.31, bf16[768,768]{1,0:T(8,128)(2,1)} %bitcast.34, f32[768,768]{1,0:T(8,128)} %ungated.1.refs_3_), custom_call_target="tpu_custom_call" | custom-call | bytes 300000 | tf_op jit(solution)/shard_map/expert/pallas_call | solution.py:190
  80.4 5.5 %all-to-all-start.2 = ((bf16[128,40,128]{2,1,0:T(8,128)(2,1)}), bf16[128,40,128]{2,1,0:T(8,128)(2,1)S(1)}, u32[]{:S(2)}, u32[]{:S(2)}) async-start(bf16[128,40,128]{2,1,0:T(8,128)(2,1)} %bitcast.33), calls=%async_computation.2 | async-start | bytes 2621440 | tf_op jit(solution)/shard_map/all_to_all | solution.py:549
  86.0 3.9 %value.1 = bf16[32,24,768]{2,1,0:T(8,128)(2,1)} custom-call(bf16[768,768]{1,0:T(8,128)(2,1)} %get-tuple-element.68.refs_0_, bf16[768,768]{1,0:T(8,128)(2,1)} %bitcast.27), custom_call_target="tpu_custom_call" | custom-call | bytes 300000 | tf_op jit(solution)/shard_map/value/pallas_call | solution.py:190
  90.2 3.9 %fusion.2 = f32[768,768]{1,0:T(8,128)} fusion(bf16[768,768]{1,0:T(8,128)(2,1)S(1)} %bitcast.32, bf16[768,768]{1,0:T(8,128)(2,1)} %get-tuple-element.70), kind=kOutput, calls=%fused_computation.4 | convolution fusion | flops 905969664 | bytes 4718592 | tf_op jit(solution)/shard_map/dot_general | solution.py:28
  94.1 2.6 %fusion = f32[768,768]{1,0:T(8,128)} fusion(bf16[768,768]{1,0:T(8,128)(2,1)S(1)} %copy-done.16, bf16[768,768]{1,0:T(8,128)(2,1)S(1)} %bitcast.30, f32[768]{0:T(1024)S(1)} %reduce), kind=kOutput, calls=%fused_computation.1 | convolution fusion | flops 907739136 | bytes 4721664 | tf_op jit(solution)/shard_map/dot_general | solution.py:28
  96.8 10.9 %all-to-all-done.2 = bf16[128,40,128]{2,1,0:T(8,128)(2,1)S(1)} async-done(((bf16[128,40,128]{2,1,0:T(8,128)(2,1)}), bf16[128,40,128]{2,1,0:T(8,128)(2,1)S(1)}, u32[]{:S(2)}, u32[]{:S(2)}) %all-to-all-start.2) | async-done | bytes 1310752 | tf_op jit(solution)/shard_map/all_to_all | solution.py:549
  107.7 4.1 %all-to-all-start.3 = ((bf16[32,24,768]{2,1,0:T(8,128)(2,1)}), bf16[32,24,768]{2,1,0:T(8,128)(2,1)S(1)}, u32[]{:S(2)}, u32[]{:S(2)}) async-start(bf16[32,24,768]{2,1,0:T(8,128)(2,1)} %value.1), calls=%async_computation.3 | async-start | bytes 2359296 | tf_op jit(solution)/shard_map/all_to_all | solution.py:545
  111.8 1.6 collect_back.1
  114.8 2.4 %collective-permute-start.7 = (bf16[768,128]{1,0:T(8,128)(2,1)S(1)}, bf16[768,128]{1,0:T(8,128)(2,1)S(1)}, u32[]{:S(2)}, u32[]{:S(2)}) collective-permute-start(bf16[768,128]{1,0:T(8,128)(2,1)S(1)} %get-tuple-element.74.refs_4_), channel_id=1, source_target_pairs={{0,2},{1,3},{2,0},{3,1},{4,6},{5,7},{6,4},{7,5},{8,10},{9,11},{10,... | collective-permute-start | bytes 589832 | tf_op jit(solution)/shard_map/ppermute | solution.py:553
  117.7 8.9 %collective-permute-done.6.refs_5_ = bf16[768,128]{1,0:T(8,128)(2,1)S(1)} collective-permute-done((bf16[768,128]{1,0:T(8,128)(2,1)S(1)}, bf16[768,128]{1,0:T(8,128)(2,1)S(1)}, u32[]{:S(2)}, u32[]{:S(2)}) %collective-permute-start.6) | collective-permute-done | bytes 196640 | tf_op jit(solution)/shard_map/ppermute | solution.py:553
  127.9 12.2 %backward.1 = (bf16[32,160,128]{2,1,0:T(8,128)(2,1)}, bf16[3,192,512]{2,1,0:T(8,128)(2,1)}, f32[1,768]{1,0:T(1,128)}, f32[128,768]{1,0:T(8,128)}) custom-call(f32[2,768]{1,0:T(2,128)} %refs_1_.3, f32[512,1]{1,0:T(8,128)} %copy-done.8, f32[512,32]{1,0:T(8,128)} %get-tuple-element.73.refs_2_, bf16[32,768]{1,0:T(8,128)(2,1)} %bitcast.37, ...), custom_call_target="tpu_custom_call" | custom-call | bytes 300000 | tf_op jit(solution)/shard_map/backward/pallas_call | solution.py:190
  140.1 1.0 copy-done.11
  141.1 7.4 %all-to-all-start.4 = ((bf16[32,160,128]{2,1,0:T(8,128)(2,1)}), bf16[32,160,128]{2,1,0:T(8,128)(2,1)S(1)}, u32[]{:S(2)}, u32[]{:S(2)}) async-start(bf16[32,160,128]{2,1,0:T(8,128)(2,1)} %get-tuple-element.92), calls=%async_computation.4 | async-start | bytes 2621440 | tf_op jit(solution)/shard_map/all_to_all | solution.py:545
  148.5 5.6 %input_grad.1 = (bf16[272,768]{1,0:T(8,128)(2,1)}, bf16[272,768]{1,0:T(8,128)(2,1)}, bf16[272,768]{1,0:T(8,128)(2,1)}, bf16[272,768]{1,0:T(8,128)(2,1)}) custom-call(f32[1,768]{1,0:T(1,128)} %get-tuple-element.85.refs_0_, s32[512,1]{1,0:T(8,128)} %get-tuple-element.64.refs_0_.refs_1_, bf16[768,768]{1,0:T(8,128)(2,1)} %bitcast.28, ...), custom_call_target="tpu_custom_call" | custom-call | bytes 300000 | tf_op jit(solution)/shard_map/input_grad/pallas_call | solution.py:190
  154.1 1.0 collective-permute-start.10
  155.1 2.0 collective-permute-start.11
  157.4 11.0 %collective-permute-done.10.refs_2_.refs_3_ = bf16[272,768]{1,0:T(8,128)(2,1)S(1)} collective-permute-done((bf16[272,768]{1,0:T(8,128)(2,1)}, bf16[272,768]{1,0:T(8,128)(2,1)S(1)}, u32[]{:S(2)}, u32[]{:S(2)}) %collective-permute-start.10) | collective-permute-done | bytes 417824 | tf_op jit(solution)/shard_map/ppermute | solution.py:553
  168.4 8.0 %collective-permute-done.11.refs_3_.refs_4_ = bf16[272,768]{1,0:T(8,128)(2,1)S(1)} collective-permute-done((bf16[272,768]{1,0:T(8,128)(2,1)}, bf16[272,768]{1,0:T(8,128)(2,1)S(1)}, u32[]{:S(2)}, u32[]{:S(2)}) %collective-permute-start.11) | collective-permute-done | bytes 417824 | tf_op jit(solution)/shard_map/ppermute | solution.py:553
  176.6 1.2 copy-done.1
  177.8 1.7 sum_gradients.1
  179.5 7.3 %all-to-all-start.5 = ((bf16[32,160,128]{2,1,0:T(8,128)(2,1)}), bf16[32,160,128]{2,1,0:T(8,128)(2,1)S(1)}, u32[]{:S(2)}, u32[]{:S(2)}) async-start(bf16[32,160,128]{2,1,0:T(8,128)(2,1)} %sum_gradients.1), calls=%async_computation.5 | async-start | bytes 2621440 | tf_op jit(solution)/shard_map/all_to_all | solution.py:545
  186.8 3.2 %token_grad.1.refs_0_ = bf16[256,768]{1,0:T(8,128)(2,1)} custom-call(f32[2,768]{1,0:T(2,128)} %refs_1_.3, bf16[272,768]{1,0:T(8,128)(2,1)} %get-tuple-element.88.refs_0_.refs_1_, bf16[272,768]{1,0:T(8,128)(2,1)} %copy-done.4, bf16[272,768]{1,0:T(8,128)(2,1)} %copy-done.2, bf16[272,768]{1,0:T(8,128)(2,1)} %copy-done.3, bf16[512,768]{1,0:T(8,128)(2,1)} %refs_5_.1, ...), custom_call_target="tpu_custom_call" | custom-call | bytes 300000 | tf_op jit(solution)/shard_map/token_grad/pallas_call | solution.py:190
  190.5 3.5 %collective-permute-start.13 = (bf16[256,768]{1,0:T(8,128)(2,1)}, bf16[256,768]{1,0:T(8,128)(2,1)S(1)}, u32[]{:S(2)}, u32[]{:S(2)}) collective-permute-start(bf16[256,768]{1,0:T(8,128)(2,1)} %token_grad.1.refs_0_), channel_id=1, source_target_pairs={{0,2},{1,3},{2,0},{3,1},{4,6},{5,7},{6,4},{7,5},{8,10},{9,11},{10,... | collective-permute-start | bytes 1179656 | tf_op jit(solution)/shard_map/ppermute | solution.py:553
  194.1 8.7 %collective-permute-done.12.refs_1_ = bf16[256,768]{1,0:T(8,128)(2,1)S(1)} collective-permute-done((bf16[256,768]{1,0:T(8,128)(2,1)}, bf16[256,768]{1,0:T(8,128)(2,1)S(1)}, u32[]{:S(2)}, u32[]{:S(2)}) %collective-permute-start.12) | collective-permute-done | bytes 393248 | tf_op jit(solution)/shard_map/ppermute | solution.py:553
  202.8 9.2 %collective-permute-done.13.refs_2_ = bf16[256,768]{1,0:T(8,128)(2,1)S(1)} collective-permute-done((bf16[256,768]{1,0:T(8,128)(2,1)}, bf16[256,768]{1,0:T(8,128)(2,1)S(1)}, u32[]{:S(2)}, u32[]{:S(2)}) %collective-permute-start.13) | collective-permute-done | bytes 393248 | tf_op jit(solution)/shard_map/ppermute | solution.py:553
  212.0 1.0 copy-done.5
  213.0 2.0 tokens.1
  215.0 1.8 finish.1
  (71 shorter events, 8.8 us)
Async XLA Ops:
  3.7 8.4 %copy-start.6 = (bf16[192,768]{1,0:T(8,128)(2,1)S(1)}, bf16[192,768]{1,0:T(8,128)(2,1)}, u32[]{:S(2)}) copy-start(bf16[192,768]{1,0:T(8,128)(2,1)} %refs_10_.1) | copy-start | bytes 884740
  3.7 14.3 %copy-start.26 = (s32[1023]{0:T(1024)S(1)}, s32[1023]{0:T(1024)}, u32[]{:S(2)}) copy-start(s32[1023]{0:T(1024)} %param.22) | copy-start | bytes 12280
  3.7 41.9 %all-to-all-start.1 = ((bf16[32,24,768]{2,1,0:T(8,128)(2,1)}), bf16[32,24,768]{2,1,0:T(8,128)(2,1)S(1)}, u32[]{:S(2)}, u32[]{:S(2)}) async-start(bf16[32,24,768]{2,1,0:T(8,128)(2,1)} %dispatch_cotangent.1), calls=%async_computation.1 | async-start | bytes 2359296 | tf_op jit(solution)/shard_map/all_to_all | solution.py:545
  12.1 15.2 %collective-permute-start.3 = (bf16[192,768]{1,0:T(8,128)(2,1)S(1)}, bf16[192,768]{1,0:T(8,128)(2,1)S(1)}, u32[]{:S(2)}, u32[]{:S(2)}) collective-permute-start(bf16[192,768]{1,0:T(8,128)(2,1)S(1)} %copy-done.6), channel_id=1, source_target_pairs={{0,1},{1,2},{2,3},{3,0},{4,5},{5,6},{6,7},{7,4},{8,9},{9,10},{10,1... | collective-permute-start | bytes 884744 | tf_op jit(solution)/shard_map/ppermute | solution.py:553
  13.8 17.0 %collective-permute-start.4 = (bf16[192,768]{1,0:T(8,128)(2,1)S(1)}, bf16[192,768]{1,0:T(8,128)(2,1)S(1)}, u32[]{:S(2)}, u32[]{:S(2)}) collective-permute-start(bf16[192,768]{1,0:T(8,128)(2,1)S(1)} %copy-done.6), channel_id=1, source_target_pairs={{0,2},{1,3},{2,0},{3,1},{4,6},{5,7},{6,4},{7,5},{8,10},{9,11},{10,... | collective-permute-start | bytes 884744 | tf_op jit(solution)/shard_map/ppermute | solution.py:553
  16.7 14.1 %collective-permute-start.5 = (bf16[192,768]{1,0:T(8,128)(2,1)S(1)}, bf16[192,768]{1,0:T(8,128)(2,1)S(1)}, u32[]{:S(2)}, u32[]{:S(2)}) collective-permute-start(bf16[192,768]{1,0:T(8,128)(2,1)S(1)} %copy-done.6), channel_id=1, source_target_pairs={{0,3},{1,0},{2,1},{3,2},{4,7},{5,4},{6,5},{7,6},{8,11},{9,8},{10,9... | collective-permute-start | bytes 884744 | tf_op jit(solution)/shard_map/ppermute | solution.py:553
  25.8 9.2 %collective-permute-start = (bf16[768,128]{1,0:T(8,128)(2,1)}, bf16[768,128]{1,0:T(8,128)(2,1)S(1)}, u32[]{:S(2)}, u32[]{:S(2)}) collective-permute-start(bf16[768,128]{1,0:T(8,128)(2,1)} %get-tuple-element.58.refs_3_), channel_id=1, source_target_pairs={{0,1},{1,2},{2,3},{3,0},{4,5},{5,6},{6,7},{7,4},{8,9},{9,10},{10,1... | collective-permute-start | bytes 589832 | tf_op jit(solution)/shard_map/ppermute | solution.py:553
  26.5 12.1 %collective-permute-start.1 = (bf16[768,128]{1,0:T(8,128)(2,1)}, bf16[768,128]{1,0:T(8,128)(2,1)S(1)}, u32[]{:S(2)}, u32[]{:S(2)}) collective-permute-start(bf16[768,128]{1,0:T(8,128)(2,1)} %get-tuple-element.58.refs_3_), channel_id=1, source_target_pairs={{0,2},{1,3},{2,0},{3,1},{4,6},{5,7},{6,4},{7,5},{8,10},{9,11},{10,... | collective-permute-start | bytes 589832 | tf_op jit(solution)/shard_map/ppermute | solution.py:553
  27.3 11.3 %collective-permute-start.2 = (bf16[768,128]{1,0:T(8,128)(2,1)}, bf16[768,128]{1,0:T(8,128)(2,1)S(1)}, u32[]{:S(2)}, u32[]{:S(2)}) collective-permute-start(bf16[768,128]{1,0:T(8,128)(2,1)} %get-tuple-element.58.refs_3_), channel_id=1, source_target_pairs={{0,3},{1,0},{2,1},{3,2},{4,7},{5,4},{6,5},{7,6},{8,11},{9,8},{10,9... | collective-permute-start | bytes 589832 | tf_op jit(solution)/shard_map/ppermute | solution.py:553
  31.4 1.0 copy-start
  35.0 3.6 %copy-start.18 = (bf16[768,128]{1,0:T(8,128)(2,1)}, bf16[768,128]{1,0:T(8,128)(2,1)S(1)}, u32[]{:S(2)}) copy-start(bf16[768,128]{1,0:T(8,128)(2,1)S(1)} %collective-permute-done.refs_4_) | copy-start | bytes 589828
  38.6 0.7 copy-start.19
  39.2 0.7 copy-start.20
  45.6 1.0 copy-start.12
  45.6 8.5 %copy-start.24 = (s32[512]{0:T(512)S(1)}, s32[512]{0:T(512)}, u32[]{:S(2)}) copy-start(s32[512]{0:T(512)} %param.20) | copy-start | bytes 6148
  45.6 9.3 %copy-start.25 = (s32[512]{0:T(512)S(1)}, s32[512]{0:T(512)}, u32[]{:S(2)}) copy-start(s32[512]{0:T(512)} %param.21) | copy-start | bytes 6148
  46.6 25.6 %all-to-all-start = ((bf16[32,24,768]{2,1,0:T(8,128)(2,1)}), bf16[32,24,768]{2,1,0:T(8,128)(2,1)S(1)}, u32[]{:S(2)}, u32[]{:S(2)}) async-start(bf16[32,24,768]{2,1,0:T(8,128)(2,1)} %get-tuple-element.59), calls=%async_computation | async-start | bytes 2359296 | tf_op jit(solution)/shard_map/all_to_all | solution.py:545
  72.3 1.0 copy-start.14
  80.4 27.3 %all-to-all-start.2 = ((bf16[128,40,128]{2,1,0:T(8,128)(2,1)}), bf16[128,40,128]{2,1,0:T(8,128)(2,1)S(1)}, u32[]{:S(2)}, u32[]{:S(2)}) async-start(bf16[128,40,128]{2,1,0:T(8,128)(2,1)} %bitcast.33), calls=%async_computation.2 | async-start | bytes 2621440 | tf_op jit(solution)/shard_map/all_to_all | solution.py:549
  86.0 4.0 %copy-start.17 = (f32[768,1]{1,0:T(8,128)S(1)}, f32[768,1]{1,0:T(8,128)}, u32[]{:S(2)}) copy-start(f32[768,1]{1,0:T(8,128)} %get-tuple-element.69) | copy-start | bytes 9220
  86.0 4.1 %copy-start.15 = (bf16[32,24,768]{2,1,0:T(8,128)(2,1)S(1)}, bf16[32,24,768]{2,1,0:T(8,128)(2,1)}, u32[]{:S(2)}) copy-start(bf16[32,24,768]{2,1,0:T(8,128)(2,1)} %copy-done.14) | copy-start | bytes 3538948
  90.2 4.0 %copy-start.13 = (bf16[32,24,768]{2,1,0:T(8,128)(2,1)S(1)}, bf16[32,24,768]{2,1,0:T(8,128)(2,1)}, u32[]{:S(2)}) copy-start(bf16[32,24,768]{2,1,0:T(8,128)(2,1)} %copy-done.12) | copy-start | bytes 3538948
  90.2 4.0 %copy-start.16 = (bf16[768,768]{1,0:T(8,128)(2,1)S(1)}, bf16[768,768]{1,0:T(8,128)(2,1)}, u32[]{:S(2)}) copy-start(bf16[768,768]{1,0:T(8,128)(2,1)} %get-tuple-element.68.refs_0_) | copy-start | bytes 3538948
  107.7 4.1 %copy-start.7 = (s32[512,1]{1,0:T(8,128)S(1)}, s32[512,1]{1,0:T(8,128)}, u32[]{:S(2)}) copy-start(s32[512,1]{1,0:T(8,128)} %get-tuple-element.64.refs_0_.refs_1_) | copy-start | bytes 6148
  107.7 32.3 %all-to-all-start.3 = ((bf16[32,24,768]{2,1,0:T(8,128)(2,1)}), bf16[32,24,768]{2,1,0:T(8,128)(2,1)S(1)}, u32[]{:S(2)}, u32[]{:S(2)}) async-start(bf16[32,24,768]{2,1,0:T(8,128)(2,1)} %value.1), calls=%async_computation.3 | async-start | bytes 2359296 | tf_op jit(solution)/shard_map/all_to_all | solution.py:545
  113.5 0.7 copy-start.8
  114.2 13.0 %copy-start.9 = (bf16[768,128]{1,0:T(8,128)(2,1)}, bf16[768,128]{1,0:T(8,128)(2,1)S(1)}, u32[]{:S(2)}) copy-start(bf16[768,128]{1,0:T(8,128)(2,1)S(1)} %get-tuple-element.74.refs_4_) | copy-start | bytes 589828
  114.2 12.4 %collective-permute-start.6 = (bf16[768,128]{1,0:T(8,128)(2,1)S(1)}, bf16[768,128]{1,0:T(8,128)(2,1)S(1)}, u32[]{:S(2)}, u32[]{:S(2)}) collective-permute-start(bf16[768,128]{1,0:T(8,128)(2,1)S(1)} %get-tuple-element.74.refs_4_), channel_id=1, source_target_pairs={{0,1},{1,2},{2,3},{3,0},{4,5},{5,6},{6,7},{7,4},{8,9},{9,10},{10,1... | collective-permute-start | bytes 589832 | tf_op jit(solution)/shard_map/ppermute | solution.py:553
  114.8 11.8 %collective-permute-start.7 = (bf16[768,128]{1,0:T(8,128)(2,1)S(1)}, bf16[768,128]{1,0:T(8,128)(2,1)S(1)}, u32[]{:S(2)}, u32[]{:S(2)}) collective-permute-start(bf16[768,128]{1,0:T(8,128)(2,1)S(1)} %get-tuple-element.74.refs_4_), channel_id=1, source_target_pairs={{0,2},{1,3},{2,0},{3,1},{4,6},{5,7},{6,4},{7,5},{8,10},{9,11},{10,... | collective-permute-start | bytes 589832 | tf_op jit(solution)/shard_map/ppermute | solution.py:553
  117.2 10.0 %collective-permute-start.8 = (bf16[768,128]{1,0:T(8,128)(2,1)S(1)}, bf16[768,128]{1,0:T(8,128)(2,1)S(1)}, u32[]{:S(2)}, u32[]{:S(2)}) collective-permute-start(bf16[768,128]{1,0:T(8,128)(2,1)S(1)} %get-tuple-element.74.refs_4_), channel_id=1, source_target_pairs={{0,3},{1,0},{2,1},{3,2},{4,7},{5,4},{6,5},{7,6},{8,11},{9,8},{10,9... | collective-permute-start | bytes 589832 | tf_op jit(solution)/shard_map/ppermute | solution.py:553
  126.6 0.7 copy-start.21
  126.6 0.7 copy-start.22
  127.2 0.7 copy-start.23
  140.0 1.0 copy-start.11
  141.1 35.5 %all-to-all-start.4 = ((bf16[32,160,128]{2,1,0:T(8,128)(2,1)}), bf16[32,160,128]{2,1,0:T(8,128)(2,1)S(1)}, u32[]{:S(2)}, u32[]{:S(2)}) async-start(bf16[32,160,128]{2,1,0:T(8,128)(2,1)} %get-tuple-element.92), calls=%async_computation.4 | async-start | bytes 2621440 | tf_op jit(solution)/shard_map/all_to_all | solution.py:545
  154.1 14.3 %collective-permute-start.10 = (bf16[272,768]{1,0:T(8,128)(2,1)}, bf16[272,768]{1,0:T(8,128)(2,1)S(1)}, u32[]{:S(2)}, u32[]{:S(2)}) collective-permute-start(bf16[272,768]{1,0:T(8,128)(2,1)} %get-tuple-element.90), channel_id=1, source_target_pairs={{0,2},{1,3},{2,0},{3,1},{4,6},{5,7},{6,4},{7,5},{8,10},{9,11},{10,... | collective-permute-start | bytes 1253384 | tf_op jit(solution)/shard_map/ppermute | solution.py:553
  155.1 21.3 %collective-permute-start.11 = (bf16[272,768]{1,0:T(8,128)(2,1)}, bf16[272,768]{1,0:T(8,128)(2,1)S(1)}, u32[]{:S(2)}, u32[]{:S(2)}) collective-permute-start(bf16[272,768]{1,0:T(8,128)(2,1)} %get-tuple-element.91), channel_id=1, source_target_pairs={{0,3},{1,0},{2,1},{3,2},{4,7},{5,4},{6,5},{7,6},{8,11},{9,8},{10,9... | collective-permute-start | bytes 1253384 | tf_op jit(solution)/shard_map/ppermute | solution.py:553
  157.1 19.5 %collective-permute-start.9 = (bf16[272,768]{1,0:T(8,128)(2,1)}, bf16[272,768]{1,0:T(8,128)(2,1)S(1)}, u32[]{:S(2)}, u32[]{:S(2)}) collective-permute-start(bf16[272,768]{1,0:T(8,128)(2,1)} %get-tuple-element.89), channel_id=1, source_target_pairs={{0,1},{1,2},{2,3},{3,0},{4,5},{5,6},{6,7},{7,4},{8,9},{9,10},{10,1... | collective-permute-start | bytes 1253384 | tf_op jit(solution)/shard_map/ppermute | solution.py:553
  168.4 11.1 %copy-start.2 = (bf16[272,768]{1,0:T(8,128)(2,1)}, bf16[272,768]{1,0:T(8,128)(2,1)S(1)}, u32[]{:S(2)}) copy-start(bf16[272,768]{1,0:T(8,128)(2,1)S(1)} %collective-permute-done.10.refs_2_.refs_3_) | copy-start | bytes 1253380
  176.4 3.1 %copy-start.3 = (bf16[272,768]{1,0:T(8,128)(2,1)}, bf16[272,768]{1,0:T(8,128)(2,1)S(1)}, u32[]{:S(2)}) copy-start(bf16[272,768]{1,0:T(8,128)(2,1)S(1)} %collective-permute-done.11.refs_3_.refs_4_) | copy-start | bytes 1253380
  176.6 2.9 %copy-start.4 = (bf16[272,768]{1,0:T(8,128)(2,1)}, bf16[272,768]{1,0:T(8,128)(2,1)S(1)}, u32[]{:S(2)}) copy-start(bf16[272,768]{1,0:T(8,128)(2,1)S(1)} %collective-permute-done.9.refs_1_.refs_2_) | copy-start | bytes 1253380
  176.6 1.2 copy-start.1
  179.5 35.4 %all-to-all-start.5 = ((bf16[32,160,128]{2,1,0:T(8,128)(2,1)}), bf16[32,160,128]{2,1,0:T(8,128)(2,1)S(1)}, u32[]{:S(2)}, u32[]{:S(2)}) async-start(bf16[32,160,128]{2,1,0:T(8,128)(2,1)} %sum_gradients.1), calls=%async_computation.5 | async-start | bytes 2621440 | tf_op jit(solution)/shard_map/all_to_all | solution.py:545
  186.8 28.2 %copy-start.10 = (f32[2,768]{1,0:T(2,128)S(1)}, f32[2,768]{1,0:T(2,128)}, u32[]{:S(2)}) copy-start(f32[2,768]{1,0:T(2,128)} %refs_1_.3) | copy-start | bytes 18436
  190.0 12.8 %collective-permute-start.12 = (bf16[256,768]{1,0:T(8,128)(2,1)}, bf16[256,768]{1,0:T(8,128)(2,1)S(1)}, u32[]{:S(2)}, u32[]{:S(2)}) collective-permute-start(bf16[256,768]{1,0:T(8,128)(2,1)} %token_grad.1.refs_0_), channel_id=1, source_target_pairs={{0,1},{1,2},{2,3},{3,0},{4,5},{5,6},{6,7},{7,4},{8,9},{9,10},{10,1... | collective-permute-start | bytes 1179656 | tf_op jit(solution)/shard_map/ppermute | solution.py:553
  190.5 21.5 %collective-permute-start.13 = (bf16[256,768]{1,0:T(8,128)(2,1)}, bf16[256,768]{1,0:T(8,128)(2,1)S(1)}, u32[]{:S(2)}, u32[]{:S(2)}) collective-permute-start(bf16[256,768]{1,0:T(8,128)(2,1)} %token_grad.1.refs_0_), channel_id=1, source_target_pairs={{0,2},{1,3},{2,0},{3,1},{4,6},{5,7},{6,4},{7,5},{8,10},{9,11},{10,... | collective-permute-start | bytes 1179656 | tf_op jit(solution)/shard_map/ppermute | solution.py:553
  194.1 17.9 %collective-permute-start.14 = (bf16[256,768]{1,0:T(8,128)(2,1)}, bf16[256,768]{1,0:T(8,128)(2,1)S(1)}, u32[]{:S(2)}, u32[]{:S(2)}) collective-permute-start(bf16[256,768]{1,0:T(8,128)(2,1)} %token_grad.1.refs_0_), channel_id=1, source_target_pairs={{0,3},{1,0},{2,1},{3,2},{4,7},{5,4},{6,5},{7,6},{8,11},{9,8},{10,9... | collective-permute-start | bytes 1179656 | tf_op jit(solution)/shard_map/ppermute | solution.py:553
  212.0 1.0 copy-start.5
where the time goes:
time: 218 us; the launch traced here: 217 us
  waiting for transfers between devices  74.6 us (34%)
  Pallas kernels  62.4 us (29%)
  starting transfers between devices  60.4 us (28%)
  local copies, waits for them, and re-layouts  10.9 us (5%)
  matrix products  6.6 us (3%)
    pallas_call x15, Pallas kernels, call(): pl.pallas_call(kernel, out_shape=outs, in_specs=in_specs, out_specs=[hbm]...  62.4 us
    ppermute x15, waiting for transfers between devices, rotate(): return lax.ppermute(v, 'shard', [(i, (i + d) % NS) for i in range(NS)])  54.3 us
    all_to_all x5, starting transfers between devices, over_experts(): return lax.all_to_all(v, 'expert', split_axis=0, concat_axis=0, tiled=True)  34.5 us
    ppermute x15, starting transfers between devices, rotate(): return lax.ppermute(v, 'shard', [(i, (i + d) % NS) for i in range(NS)])  20.3 us
    all_to_all x1, waiting for transfers between devices, over_all(): lax.all_to_all(v, ('expert', 'shard'), split_axis=0, concat_axis=0, tiled...  10.9 us
    all_to_all x5, waiting for transfers between devices, over_experts(): return lax.all_to_all(v, 'expert', split_axis=0, concat_axis=0, tiled=True)  9.36 us
    unnamed x56, local copies, waits for them, and re-layouts  9.18 us
    dot_general x2, matrix products, dot(): return lax.dot_general(a, b, dims, preferred_element_type=f32)  6.6 us
  transfers between devices with their start and end apart: 21, of which 12 were waited for; matrix products, arithmetic and copies ran while one was open for 4% of the time, Pallas kernels for 22%

commit v1 on v0

--- a/solution.py
+++ b/solution.py
@@ -46,7 +46,8 @@
 class Pieces:
     def __init__(self, arrays, first=0, rows=None):
         self.arrays = arrays
-        self.first, self.rows = first, arrays[0].shape[0] if rows is None else rows
+        self.first = first if isinstance(first, tuple) else (first,) * NS
+        self.rows = arrays[0].shape[0] if rows is None else rows
 
 
 class Hold:
@@ -153,9 +154,8 @@
                 continue
             if isinstance(a, Pieces):
                 held, sems = next(bufs), next(bufs)
-                cut = pl.ds(a.first, a.rows)
                 item = Load(held, [
-                    pltpu.make_async_copy(next(ins).at[cut], held.at[lax.rem(me[0] + (NS - d), NS)], sems.at[d])
+                    pltpu.make_async_copy(next(ins).at[pl.ds(a.first[d], a.rows)], held.at[lax.rem(me[0] + (NS - d), NS)], sems.at[d])
                     for d in range(NS)
                 ])
             elif isinstance(a, Parts):
@@ -481,13 +481,14 @@
     gain_out[...] = gain_one
 
 
-def input_grad_body(me, gain, index, got, d_proj, w, da0, da1, da2, da3, grads, values):
+def input_grad_body(me, gain, index, got, d_proj, w, da0, da1, da2, da3, own, grads, values):
     hot = (index[...] == lanes((T, SLOTS))).astype(b16)
     values[...] = dot(hot, got[...])
     grads[...] = dot(d_proj[0], w[0], TN) + dot(d_proj[1], w[1], TN) + dot(d_proj[2], w[2], TN)
     one = gain[...]
     hi = one.astype(b16).astype(f32)
     gl = jnp.concatenate([hi, one - hi, jnp.zeros((14, D), f32)], axis=0).astype(b16)
+    own[...] = gl
     for d, out in enumerate((da0, da1, da2, da3)):
         to = pl.ds(pl.multiple_of(lax.rem(me[0] + d, NS) * 128, 128), 128)
         out[:128] = grads[to, :].astype(b16)
@@ -615,8 +616,8 @@
     )
     pay, value, d_proj, gain_one = together((pay, value, d_proj, gain_one))
     pay = over_experts(pay)
-    da = call(
-        input_grad_body, [((272, D), b16)] * NS, me, gain_one, index, value, d_proj, w_t, name="input_grad",
+    *da, own = call(
+        input_grad_body, [((272, D), b16)] * NS + [((16, D), b16)], me, gain_one, index, value, d_proj, w_t, name="input_grad",
         scratch=[pltpu.VMEM((T, D), f32), pltpu.VMEM((T, D), f32)],
     )
     da = [da[0]] + [rotate(x, d) for d, x in enumerate(da) if d]
@@ -624,7 +625,7 @@
         token_grad_body, [((256, D), b16)], me, gains, Pieces(da), Quarter(tokens), d_hidden,
         Quarter(gate), Quarter(hidden), name="token_grad",
     )
-    (chunk,) = call(sum_body, [((NE, PAY, 128), b16)], me, Pieces(da, 128, 16), pay, name="sum_gradients", room=25)
+    (chunk,) = call(sum_body, [((NE, PAY, 128), b16)], me, Pieces([own] + da[1:], (0, 128, 128, 128), 16), pay, name="sum_gradients", room=25)
     chunk = over_experts(chunk)
     result, grad_tokens = call(
         tokens_body, [((T, D), b16), ((T, D), b16)], me, Pieces(round_shard(t_piece)), name="tokens", room=25,

time: 218 us -> 218 us (level)
  transfers between devices with their start and end apart: 21 -> 21, of which waited for: 12 -> 12; matrix products, arithmetic and copies ran while one was open for 4% -> 4% of each run, Pallas kernels for 22% -> 23%
where the time goes in v1:
time: 218 us; the launch traced here: 217 us
  waiting for transfers between devices  74.6 us (34%)
  Pallas kernels  62.5 us (29%)
  starting transfers between devices  60.3 us (28%)
  local copies, waits for them, and re-layouts  10.5 us (5%)
  matrix products  6.6 us (3%)
    pallas_call x15, Pallas kernels, call(): pl.pallas_call(kernel, out_shape=outs, in_specs=in_specs, out_specs=[hbm]...  62.5 us
    ppermute x15, waiting for transfers between devices, rotate(): return lax.ppermute(v, 'shard', [(i, (i + d) % NS) for i in range(NS)])  54.3 us
    all_to_all x5, starting transfers between devices, over_experts(): return lax.all_to_all(v, 'expert', split_axis=0, concat_axis=0, tiled=True)  34.5 us
    ppermute x15, starting transfers between devices, rotate(): return lax.ppermute(v, 'shard', [(i, (i + d) % NS) for i in range(NS)])  20.2 us
    all_to_all x1, waiting for transfers between devices, over_all(): lax.all_to_all(v, ('expert', 'shard'), split_axis=0, concat_axis=0, tiled...  10.9 us
    all_to_all x5, waiting for transfers between devices, over_experts(): return lax.all_to_all(v, 'expert', split_axis=0, concat_axis=0, tiled=True)  9.36 us
    unnamed x56, local copies, waits for them, and re-layouts  8.78 us
    dot_general x2, matrix products, dot(): return lax.dot_general(a, b, dims, preferred_element_type=f32)  6.6 us
  transfers between devices with their start and end apart: 21, of which 12 were waited for; matrix products, arithmetic and copies ran while one was open for 4% of the time, Pallas kernels for 23%

profile of v1, /device:TPU:0, one launch (start us, length us, event | category | flops | bytes accessed | tf_op | source)
XLA Modules:
  0.0 216.5 jit_solution(13608105183917017339)
XLA Ops:
  0.6 3.0 %dispatch_cotangent.1 = bf16[32,24,768]{2,1,0:T(8,128)(2,1)} custom-call(s32[1,512]{1,0:T(1,128)} %bitcast.40, s32[1,512]{1,0:T(1,128)} %bitcast.43, bf16[512,768]{1,0:T(8,128)(2,1)} %refs_9_.1), custom_call_target="tpu_custom_call" | custom-call | bytes 300000 | tf_op jit(solution)/shard_map/dispatch_cotangent/pallas_call | solution.py:190
  3.7 8.4 %all-to-all-start.1 = ((bf16[32,24,768]{2,1,0:T(8,128)(2,1)}), bf16[32,24,768]{2,1,0:T(8,128)(2,1)S(1)}, u32[]{:S(2)}, u32[]{:S(2)}) async-start(bf16[32,24,768]{2,1,0:T(8,128)(2,1)} %dispatch_cotangent.1), calls=%async_computation.1 | async-start | bytes 2359296 | tf_op jit(solution)/shard_map/all_to_all | solution.py:546
  12.1 1.6 collective-permute-start.3
  13.8 2.9 %collective-permute-start.4 = (bf16[192,768]{1,0:T(8,128)(2,1)S(1)}, bf16[192,768]{1,0:T(8,128)(2,1)S(1)}, u32[]{:S(2)}, u32[]{:S(2)}) collective-permute-start(bf16[192,768]{1,0:T(8,128)(2,1)S(1)} %copy-done.5), channel_id=1, source_target_pairs={{0,2},{1,3},{2,0},{3,1},{4,6},{5,7},{6,4},{7,5},{8,10},{9,11},{10,... | collective-permute-start | bytes 884744 | tf_op jit(solution)/shard_map/ppermute | solution.py:554
  16.7 1.3 collective-permute-start.5
  18.8 6.9 %attend.1 = (bf16[768,128]{1,0:T(8,128)(2,1)}, bf16[192,512]{1,0:T(8,128)(2,1)}, bf16[512,768]{1,0:T(8,128)(2,1)}, bf16[2,192,512]{2,1,0:T(8,128)(2,1)}, bf16[51...) custom-call(bf16[512,768]{1,0:T(8,128)(2,1)} %refs_5_.1, f32[2,768]{1,0:T(2,128)} %refs_1_.3, bf16[3,192,768]{2,1,0:T(8,128)(2,1)} %bitcast.23, ...), custom_call_target="tpu_custom_call" | custom-call | bytes 300000 | tf_op jit(solution)/shard_map/attend/pallas_call | solution.py:190
  26.5 0.8 collective-permute-start.1
  27.3 2.0 collective-permute-start.2
  29.3 1.5 collective-permute-done.4.refs_2_
  31.5 1.0 copy-done
  32.5 2.5 %collective-permute-done.refs_4_ = bf16[768,128]{1,0:T(8,128)(2,1)S(1)} collective-permute-done((bf16[768,128]{1,0:T(8,128)(2,1)}, bf16[768,128]{1,0:T(8,128)(2,1)S(1)}, u32[]{:S(2)}, u32[]{:S(2)}) %collective-permute-start) | collective-permute-done | bytes 196640 | tf_op jit(solution)/shard_map/ppermute | solution.py:554
  35.0 3.6 %collective-permute-done.1.refs_5_ = bf16[768,128]{1,0:T(8,128)(2,1)S(1)} collective-permute-done((bf16[768,128]{1,0:T(8,128)(2,1)}, bf16[768,128]{1,0:T(8,128)(2,1)S(1)}, u32[]{:S(2)}, u32[]{:S(2)}) %collective-permute-start.1) | collective-permute-done | bytes 196640 | tf_op jit(solution)/shard_map/ppermute | solution.py:554
  39.9 5.7 %mix.1 = (bf16[32,24,768]{2,1,0:T(8,128)(2,1)}, bf16[512,768]{1,0:T(8,128)(2,1)}, f32[512,768]{1,0:T(8,128)}) custom-call(s32[1,512]{1,0:T(1,128)} %bitcast.41, s32[1,512]{1,0:T(1,128)} %bitcast.44, f32[2,768]{1,0:T(2,128)} %refs_1_.3, bf16[768,128]{1,0:T(8,128)(2,1)} %get-tuple-element.59.refs_3_, bf16[768,128]{1,0:T(8,128)(2,1)} %copy-done.18, ...), custom_call_target="tpu_custom_call" | custom-call | bytes 300000 | tf_op jit(solution)/shard_map/mix/pallas_call | solution.py:190
  45.6 1.0 copy-done.12
  46.6 7.4 %all-to-all-start = ((bf16[32,24,768]{2,1,0:T(8,128)(2,1)}), bf16[32,24,768]{2,1,0:T(8,128)(2,1)S(1)}, u32[]{:S(2)}, u32[]{:S(2)}) async-start(bf16[32,24,768]{2,1,0:T(8,128)(2,1)} %get-tuple-element.60), calls=%async_computation | async-start | bytes 2359296 | tf_op jit(solution)/shard_map/all_to_all | solution.py:546
  54.1 0.9 copy.21.refs_2_
  54.9 0.9 copy.22.refs_3_
  55.8 2.9 %gate.1 = (f32[512,1]{1,0:T(8,128)}, f32[512,32]{1,0:T(8,128)}, s32[512,1]{1,0:T(8,128)}) custom-call(bf16[512,768]{1,0:T(8,128)(2,1)} %get-tuple-element.61.refs_0_.refs_15_, bf16[32,768]{1,0:T(8,128)(2,1)} %bitcast.35, s32[512,1]{1,0:T(8,128)} %copy.21.refs_2_, s32[512,1]{1,0:T(8,128)} %copy.22.refs_3_), custom_call_target="tpu_custom_call" | custom-call | bytes 300000 | tf_op jit(solution)/shard_map/gate/pallas_call | solution.py:190
  58.7 4.2 %ungated.1.refs_3_ = f32[768,768]{1,0:T(8,128)} custom-call(bf16[768,768]{1,0:T(8,128)(2,1)} %bitcast.29, bf16[768,768]{1,0:T(8,128)(2,1)} %bitcast.26), custom_call_target="tpu_custom_call" | custom-call | bytes 300000 | tf_op jit(solution)/shard_map/ungated/pallas_call | solution.py:190
  62.9 9.3 %all-to-all-done = bf16[32,24,768]{2,1,0:T(8,128)(2,1)S(1)} async-done(((bf16[32,24,768]{2,1,0:T(8,128)(2,1)}), bf16[32,24,768]{2,1,0:T(8,128)(2,1)S(1)}, u32[]{:S(2)}, u32[]{:S(2)}) %all-to-all-start) | async-done | bytes 1179680 | tf_op jit(solution)/shard_map/all_to_all | solution.py:546
  72.3 1.0 copy-done.14
  73.3 7.2 %expert.1 = (bf16[32,4,40,128]{3,2,1,0:T(8,128)(2,1)}, bf16[768,768]{1,0:T(8,128)(2,1)}, bf16[768,768]{1,0:T(8,128)(2,1)}, f32[768,1]{1,0:T(8,128)}) custom-call(bf16[32,768]{1,0:T(8,128)(2,1)} %bitcast.36, bf16[768,768]{1,0:T(8,128)(2,1)} %bitcast.31, bf16[768,768]{1,0:T(8,128)(2,1)} %bitcast.34, f32[768,768]{1,0:T(8,128)} %ungated.1.refs_3_), custom_call_target="tpu_custom_call" | custom-call | bytes 300000 | tf_op jit(solution)/shard_map/expert/pallas_call | solution.py:190
  80.4 5.6 %all-to-all-start.2 = ((bf16[128,40,128]{2,1,0:T(8,128)(2,1)}), bf16[128,40,128]{2,1,0:T(8,128)(2,1)S(1)}, u32[]{:S(2)}, u32[]{:S(2)}) async-start(bf16[128,40,128]{2,1,0:T(8,128)(2,1)} %bitcast.33), calls=%async_computation.2 | async-start | bytes 2621440 | tf_op jit(solution)/shard_map/all_to_all | solution.py:550
  86.0 3.9 %value.1 = bf16[32,24,768]{2,1,0:T(8,128)(2,1)} custom-call(bf16[768,768]{1,0:T(8,128)(2,1)} %get-tuple-element.69.refs_0_, bf16[768,768]{1,0:T(8,128)(2,1)} %bitcast.27), custom_call_target="tpu_custom_call" | custom-call | bytes 300000 | tf_op jit(solution)/shard_map/value/pallas_call | solution.py:190
  90.2 3.9 %fusion.2 = f32[768,768]{1,0:T(8,128)} fusion(bf16[768,768]{1,0:T(8,128)(2,1)S(1)} %bitcast.32, bf16[768,768]{1,0:T(8,128)(2,1)} %get-tuple-element.71), kind=kOutput, calls=%fused_computation.4 | convolution fusion | flops 905969664 | bytes 4718592 | tf_op jit(solution)/shard_map/dot_general | solution.py:28
  94.1 2.6 %fusion = f32[768,768]{1,0:T(8,128)} fusion(bf16[768,768]{1,0:T(8,128)(2,1)S(1)} %copy-done.16, bf16[768,768]{1,0:T(8,128)(2,1)S(1)} %bitcast.30, f32[768]{0:T(1024)S(1)} %reduce), kind=kOutput, calls=%fused_computation.1 | convolution fusion | flops 907739136 | bytes 4721664 | tf_op jit(solution)/shard_map/dot_general | solution.py:28
  96.8 10.9 %all-to-all-done.2 = bf16[128,40,128]{2,1,0:T(8,128)(2,1)S(1)} async-done(((bf16[128,40,128]{2,1,0:T(8,128)(2,1)}), bf16[128,40,128]{2,1,0:T(8,128)(2,1)S(1)}, u32[]{:S(2)}, u32[]{:S(2)}) %all-to-all-start.2) | async-done | bytes 1310752 | tf_op jit(solution)/shard_map/all_to_all | solution.py:550
  107.7 4.1 %all-to-all-start.3 = ((bf16[32,24,768]{2,1,0:T(8,128)(2,1)}), bf16[32,24,768]{2,1,0:T(8,128)(2,1)S(1)}, u32[]{:S(2)}, u32[]{:S(2)}) async-start(bf16[32,24,768]{2,1,0:T(8,128)(2,1)} %value.1), calls=%async_computation.3 | async-start | bytes 2359296 | tf_op jit(solution)/shard_map/all_to_all | solution.py:546
  111.8 1.6 collect_back.1
  114.8 2.4 %collective-permute-start.7 = (bf16[768,128]{1,0:T(8,128)(2,1)S(1)}, bf16[768,128]{1,0:T(8,128)(2,1)S(1)}, u32[]{:S(2)}, u32[]{:S(2)}) collective-permute-start(bf16[768,128]{1,0:T(8,128)(2,1)S(1)} %get-tuple-element.75.refs_4_), channel_id=1, source_target_pairs={{0,2},{1,3},{2,0},{3,1},{4,6},{5,7},{6,4},{7,5},{8,10},{9,11},{10,... | collective-permute-start | bytes 589832 | tf_op jit(solution)/shard_map/ppermute | solution.py:554
  117.7 8.9 %collective-permute-done.6.refs_5_ = bf16[768,128]{1,0:T(8,128)(2,1)S(1)} collective-permute-done((bf16[768,128]{1,0:T(8,128)(2,1)S(1)}, bf16[768,128]{1,0:T(8,128)(2,1)S(1)}, u32[]{:S(2)}, u32[]{:S(2)}) %collective-permute-start.6) | collective-permute-done | bytes 196640 | tf_op jit(solution)/shard_map/ppermute | solution.py:554
  127.9 12.1 %backward.1 = (bf16[32,160,128]{2,1,0:T(8,128)(2,1)}, bf16[3,192,512]{2,1,0:T(8,128)(2,1)}, f32[1,768]{1,0:T(1,128)}, f32[128,768]{1,0:T(8,128)}) custom-call(f32[2,768]{1,0:T(2,128)} %refs_1_.3, f32[512,1]{1,0:T(8,128)} %copy-done.7, f32[512,32]{1,0:T(8,128)} %get-tuple-element.74.refs_2_, bf16[32,768]{1,0:T(8,128)(2,1)} %bitcast.37, ...), custom_call_target="tpu_custom_call" | custom-call | bytes 300000 | tf_op jit(solution)/shard_map/backward/pallas_call | solution.py:190
  140.1 1.0 copy-done.11
  141.1 7.4 %all-to-all-start.4 = ((bf16[32,160,128]{2,1,0:T(8,128)(2,1)}), bf16[32,160,128]{2,1,0:T(8,128)(2,1)S(1)}, u32[]{:S(2)}, u32[]{:S(2)}) async-start(bf16[32,160,128]{2,1,0:T(8,128)(2,1)} %get-tuple-element.93), calls=%async_computation.4 | async-start | bytes 2621440 | tf_op jit(solution)/shard_map/all_to_all | solution.py:546
  148.5 5.6 %input_grad.1 = (bf16[272,768]{1,0:T(8,128)(2,1)}, bf16[272,768]{1,0:T(8,128)(2,1)}, bf16[272,768]{1,0:T(8,128)(2,1)}, bf16[272,768]{1,0:T(8,128)(2,1)}, bf16[16,768]{1,0:T(8,128)(2,1)}) custom-call(f32[1,768]{1,0:T(1,128)} %get-tuple-element.86.refs_0_, s32[512,1]{1,0:T(8,128)} %get-tuple-element.65.refs_0_.refs_1_, bf16[768,768]{1,0:T(8,128)(2,1)} %bitcast.28, ...), custom_call_target="tpu_custom_call" | custom-call | bytes 300000 | tf_op jit(solution)/shard_map/input_grad/pallas_call | solution.py:190
  154.1 1.0 collective-permute-start.10
  155.1 2.0 collective-permute-start.11
  157.5 11.0 %collective-permute-done.10.refs_2_.refs_3_ = bf16[272,768]{1,0:T(8,128)(2,1)S(1)} collective-permute-done((bf16[272,768]{1,0:T(8,128)(2,1)}, bf16[272,768]{1,0:T(8,128)(2,1)S(1)}, u32[]{:S(2)}, u32[]{:S(2)}) %collective-permute-start.10) | collective-permute-done | bytes 417824 | tf_op jit(solution)/shard_map/ppermute | solution.py:554
  168.4 8.0 %collective-permute-done.11.refs_3_.refs_4_ = bf16[272,768]{1,0:T(8,128)(2,1)S(1)} collective-permute-done((bf16[272,768]{1,0:T(8,128)(2,1)}, bf16[272,768]{1,0:T(8,128)(2,1)S(1)}, u32[]{:S(2)}, u32[]{:S(2)}) %collective-permute-start.11) | collective-permute-done | bytes 417824 | tf_op jit(solution)/shard_map/ppermute | solution.py:554
  177.4 1.7 sum_gradients.1
  179.2 7.3 %all-to-all-start.5 = ((bf16[32,160,128]{2,1,0:T(8,128)(2,1)}), bf16[32,160,128]{2,1,0:T(8,128)(2,1)S(1)}, u32[]{:S(2)}, u32[]{:S(2)}) async-start(bf16[32,160,128]{2,1,0:T(8,128)(2,1)} %sum_gradients.1), calls=%async_computation.5 | async-start | bytes 2621440 | tf_op jit(solution)/shard_map/all_to_all | solution.py:546
  186.5 3.2 %token_grad.1.refs_0_ = bf16[256,768]{1,0:T(8,128)(2,1)} custom-call(f32[2,768]{1,0:T(2,128)} %refs_1_.3, bf16[272,768]{1,0:T(8,128)(2,1)} %get-tuple-element.94.refs_1_, bf16[272,768]{1,0:T(8,128)(2,1)} %copy-done.3, bf16[272,768]{1,0:T(8,128)(2,1)} %copy-done.1, bf16[272,768]{1,0:T(8,128)(2,1)} %copy-done.2, bf16[512,768]{1,0:T(8,128)(2,1)} %refs_5_.1, ...), custom_call_target="tpu_custom_call" | custom-call | bytes 300000 | tf_op jit(solution)/shard_map/token_grad/pallas_call | solution.py:190
  190.1 3.6 %collective-permute-start.13 = (bf16[256,768]{1,0:T(8,128)(2,1)}, bf16[256,768]{1,0:T(8,128)(2,1)S(1)}, u32[]{:S(2)}, u32[]{:S(2)}) collective-permute-start(bf16[256,768]{1,0:T(8,128)(2,1)} %token_grad.1.refs_0_), channel_id=1, source_target_pairs={{0,2},{1,3},{2,0},{3,1},{4,6},{5,7},{6,4},{7,5},{8,10},{9,11},{10,... | collective-permute-start | bytes 1179656 | tf_op jit(solution)/shard_map/ppermute | solution.py:554
  193.6 8.8 %collective-permute-done.12.refs_1_ = bf16[256,768]{1,0:T(8,128)(2,1)S(1)} collective-permute-done((bf16[256,768]{1,0:T(8,128)(2,1)}, bf16[256,768]{1,0:T(8,128)(2,1)S(1)}, u32[]{:S(2)}, u32[]{:S(2)}) %collective-permute-start.12) | collective-permute-done | bytes 393248 | tf_op jit(solution)/shard_map/ppermute | solution.py:554
  202.4 9.1 %collective-permute-done.13.refs_2_ = bf16[256,768]{1,0:T(8,128)(2,1)S(1)} collective-permute-done((bf16[256,768]{1,0:T(8,128)(2,1)}, bf16[256,768]{1,0:T(8,128)(2,1)S(1)}, u32[]{:S(2)}, u32[]{:S(2)}) %collective-permute-start.13) | collective-permute-done | bytes 393248 | tf_op jit(solution)/shard_map/ppermute | solution.py:554
  211.5 1.0 copy-done.4
  212.5 2.0 tokens.1
  214.5 1.8 finish.1
  (71 shorter events, 8.7 us)
Async XLA Ops:
  3.7 8.4 %copy-start.5 = (bf16[192,768]{1,0:T(8,128)(2,1)S(1)}, bf16[192,768]{1,0:T(8,128)(2,1)}, u32[]{:S(2)}) copy-start(bf16[192,768]{1,0:T(8,128)(2,1)} %refs_10_.1) | copy-start | bytes 884740
  3.7 14.3 %copy-start.26 = (s32[1023]{0:T(1024)S(1)}, s32[1023]{0:T(1024)}, u32[]{:S(2)}) copy-start(s32[1023]{0:T(1024)} %param.22) | copy-start | bytes 12280
  3.7 41.9 %all-to-all-start.1 = ((bf16[32,24,768]{2,1,0:T(8,128)(2,1)}), bf16[32,24,768]{2,1,0:T(8,128)(2,1)S(1)}, u32[]{:S(2)}, u32[]{:S(2)}) async-start(bf16[32,24,768]{2,1,0:T(8,128)(2,1)} %dispatch_cotangent.1), calls=%async_computation.1 | async-start | bytes 2359296 | tf_op jit(solution)/shard_map/all_to_all | solution.py:546
  12.1 15.2 %collective-permute-start.3 = (bf16[192,768]{1,0:T(8,128)(2,1)S(1)}, bf16[192,768]{1,0:T(8,128)(2,1)S(1)}, u32[]{:S(2)}, u32[]{:S(2)}) collective-permute-start(bf16[192,768]{1,0:T(8,128)(2,1)S(1)} %copy-done.5), channel_id=1, source_target_pairs={{0,1},{1,2},{2,3},{3,0},{4,5},{5,6},{6,7},{7,4},{8,9},{9,10},{10,1... | collective-permute-start | bytes 884744 | tf_op jit(solution)/shard_map/ppermute | solution.py:554
  13.8 17.0 %collective-permute-start.4 = (bf16[192,768]{1,0:T(8,128)(2,1)S(1)}, bf16[192,768]{1,0:T(8,128)(2,1)S(1)}, u32[]{:S(2)}, u32[]{:S(2)}) collective-permute-start(bf16[192,768]{1,0:T(8,128)(2,1)S(1)} %copy-done.5), channel_id=1, source_target_pairs={{0,2},{1,3},{2,0},{3,1},{4,6},{5,7},{6,4},{7,5},{8,10},{9,11},{10,... | collective-permute-start | bytes 884744 | tf_op jit(solution)/shard_map/ppermute | solution.py:554
  16.7 14.1 %collective-permute-start.5 = (bf16[192,768]{1,0:T(8,128)(2,1)S(1)}, bf16[192,768]{1,0:T(8,128)(2,1)S(1)}, u32[]{:S(2)}, u32[]{:S(2)}) collective-permute-start(bf16[192,768]{1,0:T(8,128)(2,1)S(1)} %copy-done.5), channel_id=1, source_target_pairs={{0,3},{1,0},{2,1},{3,2},{4,7},{5,4},{6,5},{7,6},{8,11},{9,8},{10,9... | collective-permute-start | bytes 884744 | tf_op jit(solution)/shard_map/ppermute | solution.py:554
  25.7 9.2 %collective-permute-start = (bf16[768,128]{1,0:T(8,128)(2,1)}, bf16[768,128]{1,0:T(8,128)(2,1)S(1)}, u32[]{:S(2)}, u32[]{:S(2)}) collective-permute-start(bf16[768,128]{1,0:T(8,128)(2,1)} %get-tuple-element.59.refs_3_), channel_id=1, source_target_pairs={{0,1},{1,2},{2,3},{3,0},{4,5},{5,6},{6,7},{7,4},{8,9},{9,10},{10,1... | collective-permute-start | bytes 589832 | tf_op jit(solution)/shard_map/ppermute | solution.py:554
  26.5 12.1 %collective-permute-start.1 = (bf16[768,128]{1,0:T(8,128)(2,1)}, bf16[768,128]{1,0:T(8,128)(2,1)S(1)}, u32[]{:S(2)}, u32[]{:S(2)}) collective-permute-start(bf16[768,128]{1,0:T(8,128)(2,1)} %get-tuple-element.59.refs_3_), channel_id=1, source_target_pairs={{0,2},{1,3},{2,0},{3,1},{4,6},{5,7},{6,4},{7,5},{8,10},{9,11},{10,... | collective-permute-start | bytes 589832 | tf_op jit(solution)/shard_map/ppermute | solution.py:554
  27.3 11.3 %collective-permute-start.2 = (bf16[768,128]{1,0:T(8,128)(2,1)}, bf16[768,128]{1,0:T(8,128)(2,1)S(1)}, u32[]{:S(2)}, u32[]{:S(2)}) collective-permute-start(bf16[768,128]{1,0:T(8,128)(2,1)} %get-tuple-element.59.refs_3_), channel_id=1, source_target_pairs={{0,3},{1,0},{2,1},{3,2},{4,7},{5,4},{6,5},{7,6},{8,11},{9,8},{10,9... | collective-permute-start | bytes 589832 | tf_op jit(solution)/shard_map/ppermute | solution.py:554
  31.4 1.0 copy-start
  35.0 3.6 %copy-start.18 = (bf16[768,128]{1,0:T(8,128)(2,1)}, bf16[768,128]{1,0:T(8,128)(2,1)S(1)}, u32[]{:S(2)}) copy-start(bf16[768,128]{1,0:T(8,128)(2,1)S(1)} %collective-permute-done.refs_4_) | copy-start | bytes 589828
  38.6 0.7 copy-start.19
  39.2 0.7 copy-start.20
  45.6 1.0 copy-start.12
  45.6 8.5 %copy-start.24 = (s32[512]{0:T(512)S(1)}, s32[512]{0:T(512)}, u32[]{:S(2)}) copy-start(s32[512]{0:T(512)} %param.20) | copy-start | bytes 6148
  45.6 9.3 %copy-start.25 = (s32[512]{0:T(512)S(1)}, s32[512]{0:T(512)}, u32[]{:S(2)}) copy-start(s32[512]{0:T(512)} %param.21) | copy-start | bytes 6148
  46.6 25.6 %all-to-all-start = ((bf16[32,24,768]{2,1,0:T(8,128)(2,1)}), bf16[32,24,768]{2,1,0:T(8,128)(2,1)S(1)}, u32[]{:S(2)}, u32[]{:S(2)}) async-start(bf16[32,24,768]{2,1,0:T(8,128)(2,1)} %get-tuple-element.60), calls=%async_computation | async-start | bytes 2359296 | tf_op jit(solution)/shard_map/all_to_all | solution.py:546
  72.3 1.0 copy-start.14
  80.4 27.3 %all-to-all-start.2 = ((bf16[128,40,128]{2,1,0:T(8,128)(2,1)}), bf16[128,40,128]{2,1,0:T(8,128)(2,1)S(1)}, u32[]{:S(2)}, u32[]{:S(2)}) async-start(bf16[128,40,128]{2,1,0:T(8,128)(2,1)} %bitcast.33), calls=%async_computation.2 | async-start | bytes 2621440 | tf_op jit(solution)/shard_map/all_to_all | solution.py:550
  86.0 4.0 %copy-start.17 = (f32[768,1]{1,0:T(8,128)S(1)}, f32[768,1]{1,0:T(8,128)}, u32[]{:S(2)}) copy-start(f32[768,1]{1,0:T(8,128)} %get-tuple-element.70) | copy-start | bytes 9220
  86.0 4.1 %copy-start.15 = (bf16[32,24,768]{2,1,0:T(8,128)(2,1)S(1)}, bf16[32,24,768]{2,1,0:T(8,128)(2,1)}, u32[]{:S(2)}) copy-start(bf16[32,24,768]{2,1,0:T(8,128)(2,1)} %copy-done.14) | copy-start | bytes 3538948
  90.2 4.0 %copy-start.13 = (bf16[32,24,768]{2,1,0:T(8,128)(2,1)S(1)}, bf16[32,24,768]{2,1,0:T(8,128)(2,1)}, u32[]{:S(2)}) copy-start(bf16[32,24,768]{2,1,0:T(8,128)(2,1)} %copy-done.12) | copy-start | bytes 3538948
  90.2 4.0 %copy-start.16 = (bf16[768,768]{1,0:T(8,128)(2,1)S(1)}, bf16[768,768]{1,0:T(8,128)(2,1)}, u32[]{:S(2)}) copy-start(bf16[768,768]{1,0:T(8,128)(2,1)} %get-tuple-element.69.refs_0_) | copy-start | bytes 3538948
  107.7 4.1 %copy-start.6 = (s32[512,1]{1,0:T(8,128)S(1)}, s32[512,1]{1,0:T(8,128)}, u32[]{:S(2)}) copy-start(s32[512,1]{1,0:T(8,128)} %get-tuple-element.65.refs_0_.refs_1_) | copy-start | bytes 6148
  107.7 32.3 %all-to-all-start.3 = ((bf16[32,24,768]{2,1,0:T(8,128)(2,1)}), bf16[32,24,768]{2,1,0:T(8,128)(2,1)S(1)}, u32[]{:S(2)}, u32[]{:S(2)}) async-start(bf16[32,24,768]{2,1,0:T(8,128)(2,1)} %value.1), calls=%async_computation.3 | async-start | bytes 2359296 | tf_op jit(solution)/shard_map/all_to_all | solution.py:546
  113.5 0.7 copy-start.7
  114.2 13.0 %copy-start.8 = (bf16[768,128]{1,0:T(8,128)(2,1)}, bf16[768,128]{1,0:T(8,128)(2,1)S(1)}, u32[]{:S(2)}) copy-start(bf16[768,128]{1,0:T(8,128)(2,1)S(1)} %get-tuple-element.75.refs_4_) | copy-start | bytes 589828
  114.2 12.4 %collective-permute-start.6 = (bf16[768,128]{1,0:T(8,128)(2,1)S(1)}, bf16[768,128]{1,0:T(8,128)(2,1)S(1)}, u32[]{:S(2)}, u32[]{:S(2)}) collective-permute-start(bf16[768,128]{1,0:T(8,128)(2,1)S(1)} %get-tuple-element.75.refs_4_), channel_id=1, source_target_pairs={{0,1},{1,2},{2,3},{3,0},{4,5},{5,6},{6,7},{7,4},{8,9},{9,10},{10,1... | collective-permute-start | bytes 589832 | tf_op jit(solution)/shard_map/ppermute | solution.py:554
  114.8 11.8 %collective-permute-start.7 = (bf16[768,128]{1,0:T(8,128)(2,1)S(1)}, bf16[768,128]{1,0:T(8,128)(2,1)S(1)}, u32[]{:S(2)}, u32[]{:S(2)}) collective-permute-start(bf16[768,128]{1,0:T(8,128)(2,1)S(1)} %get-tuple-element.75.refs_4_), channel_id=1, source_target_pairs={{0,2},{1,3},{2,0},{3,1},{4,6},{5,7},{6,4},{7,5},{8,10},{9,11},{10,... | collective-permute-start | bytes 589832 | tf_op jit(solution)/shard_map/ppermute | solution.py:554
  117.2 10.0 %collective-permute-start.8 = (bf16[768,128]{1,0:T(8,128)(2,1)S(1)}, bf16[768,128]{1,0:T(8,128)(2,1)S(1)}, u32[]{:S(2)}, u32[]{:S(2)}) collective-permute-start(bf16[768,128]{1,0:T(8,128)(2,1)S(1)} %get-tuple-element.75.refs_4_), channel_id=1, source_target_pairs={{0,3},{1,0},{2,1},{3,2},{4,7},{5,4},{6,5},{7,6},{8,11},{9,8},{10,9... | collective-permute-start | bytes 589832 | tf_op jit(solution)/shard_map/ppermute | solution.py:554
  126.6 0.7 copy-start.21
  126.6 0.7 copy-start.22
  127.2 0.7 copy-start.23
  140.0 1.0 copy-start.11
  141.1 35.6 %all-to-all-start.4 = ((bf16[32,160,128]{2,1,0:T(8,128)(2,1)}), bf16[32,160,128]{2,1,0:T(8,128)(2,1)S(1)}, u32[]{:S(2)}, u32[]{:S(2)}) async-start(bf16[32,160,128]{2,1,0:T(8,128)(2,1)} %get-tuple-element.93), calls=%async_computation.4 | async-start | bytes 2621440 | tf_op jit(solution)/shard_map/all_to_all | solution.py:546
  154.1 14.3 %collective-permute-start.10 = (bf16[272,768]{1,0:T(8,128)(2,1)}, bf16[272,768]{1,0:T(8,128)(2,1)S(1)}, u32[]{:S(2)}, u32[]{:S(2)}) collective-permute-start(bf16[272,768]{1,0:T(8,128)(2,1)} %get-tuple-element.91), channel_id=1, source_target_pairs={{0,2},{1,3},{2,0},{3,1},{4,6},{5,7},{6,4},{7,5},{8,10},{9,11},{10,... | collective-permute-start | bytes 1253384 | tf_op jit(solution)/shard_map/ppermute | solution.py:554
  155.1 21.3 %collective-permute-start.11 = (bf16[272,768]{1,0:T(8,128)(2,1)}, bf16[272,768]{1,0:T(8,128)(2,1)S(1)}, u32[]{:S(2)}, u32[]{:S(2)}) collective-permute-start(bf16[272,768]{1,0:T(8,128)(2,1)} %get-tuple-element.92), channel_id=1, source_target_pairs={{0,3},{1,0},{2,1},{3,2},{4,7},{5,4},{6,5},{7,6},{8,11},{9,8},{10,9... | collective-permute-start | bytes 1253384 | tf_op jit(solution)/shard_map/ppermute | solution.py:554
  157.2 19.5 %collective-permute-start.9 = (bf16[272,768]{1,0:T(8,128)(2,1)}, bf16[272,768]{1,0:T(8,128)(2,1)S(1)}, u32[]{:S(2)}, u32[]{:S(2)}) collective-permute-start(bf16[272,768]{1,0:T(8,128)(2,1)} %get-tuple-element.90), channel_id=1, source_target_pairs={{0,1},{1,2},{2,3},{3,0},{4,5},{5,6},{6,7},{7,4},{8,9},{9,10},{10,1... | collective-permute-start | bytes 1253384 | tf_op jit(solution)/shard_map/ppermute | solution.py:554
  168.4 10.8 %copy-start.1 = (bf16[272,768]{1,0:T(8,128)(2,1)}, bf16[272,768]{1,0:T(8,128)(2,1)S(1)}, u32[]{:S(2)}) copy-start(bf16[272,768]{1,0:T(8,128)(2,1)S(1)} %collective-permute-done.10.refs_2_.refs_3_) | copy-start | bytes 1253380
  176.5 2.7 %copy-start.2 = (bf16[272,768]{1,0:T(8,128)(2,1)}, bf16[272,768]{1,0:T(8,128)(2,1)S(1)}, u32[]{:S(2)}) copy-start(bf16[272,768]{1,0:T(8,128)(2,1)S(1)} %collective-permute-done.11.refs_3_.refs_4_) | copy-start | bytes 1253380
  176.7 2.5 %copy-start.3 = (bf16[272,768]{1,0:T(8,128)(2,1)}, bf16[272,768]{1,0:T(8,128)(2,1)S(1)}, u32[]{:S(2)}) copy-start(bf16[272,768]{1,0:T(8,128)(2,1)S(1)} %collective-permute-done.9.refs_1_.refs_2_) | copy-start | bytes 1253380
  176.7 0.8 copy-start.10
  179.2 35.3 %all-to-all-start.5 = ((bf16[32,160,128]{2,1,0:T(8,128)(2,1)}), bf16[32,160,128]{2,1,0:T(8,128)(2,1)S(1)}, u32[]{:S(2)}, u32[]{:S(2)}) async-start(bf16[32,160,128]{2,1,0:T(8,128)(2,1)} %sum_gradients.1), calls=%async_computation.5 | async-start | bytes 2621440 | tf_op jit(solution)/shard_map/all_to_all | solution.py:546
  186.5 28.0 %copy-start.9 = (f32[2,768]{1,0:T(2,128)S(1)}, f32[2,768]{1,0:T(2,128)}, u32[]{:S(2)}) copy-start(f32[2,768]{1,0:T(2,128)} %refs_1_.3) | copy-start | bytes 18436
  189.7 12.8 %collective-permute-start.12 = (bf16[256,768]{1,0:T(8,128)(2,1)}, bf16[256,768]{1,0:T(8,128)(2,1)S(1)}, u32[]{:S(2)}, u32[]{:S(2)}) collective-permute-start(bf16[256,768]{1,0:T(8,128)(2,1)} %token_grad.1.refs_0_), channel_id=1, source_target_pairs={{0,1},{1,2},{2,3},{3,0},{4,5},{5,6},{6,7},{7,4},{8,9},{9,10},{10,1... | collective-permute-start | bytes 1179656 | tf_op jit(solution)/shard_map/ppermute | solution.py:554
  190.1 21.5 %collective-permute-start.13 = (bf16[256,768]{1,0:T(8,128)(2,1)}, bf16[256,768]{1,0:T(8,128)(2,1)S(1)}, u32[]{:S(2)}, u32[]{:S(2)}) collective-permute-start(bf16[256,768]{1,0:T(8,128)(2,1)} %token_grad.1.refs_0_), channel_id=1, source_target_pairs={{0,2},{1,3},{2,0},{3,1},{4,6},{5,7},{6,4},{7,5},{8,10},{9,11},{10,... | collective-permute-start | bytes 1179656 | tf_op jit(solution)/shard_map/ppermute | solution.py:554
  193.6 17.9 %collective-permute-start.14 = (bf16[256,768]{1,0:T(8,128)(2,1)}, bf16[256,768]{1,0:T(8,128)(2,1)S(1)}, u32[]{:S(2)}, u32[]{:S(2)}) collective-permute-start(bf16[256,768]{1,0:T(8,128)(2,1)} %token_grad.1.refs_0_), channel_id=1, source_target_pairs={{0,3},{1,0},{2,1},{3,2},{4,7},{5,4},{6,5},{7,6},{8,11},{9,8},{10,9... | collective-permute-start | bytes 1179656 | tf_op jit(solution)/shard_map/ppermute | solution.py:554
  211.5 1.0 copy-start.4
